TPU v7x, 128 devices: a whole 4x4x4 slice. The times are simulated.
128 devices in a mesh: ty: 8 (over y, x_lo), tx: 16 (over x_hi, z, core).
Axes of the slice: x: 4 (x_hi: 2, x_lo: 2; x = x_hi * 2 + x_lo), y: 4, z: 4, core: 2. Of those that a mesh axis runs over, the one named last changes fastest.
Arguments:
- features: bfloat16 [256, 12, 128, 128], P(('ty', 'tx')), may hold values from -6 to 6
- conv_kernel: float32 [49, 256], P(None, ('ty', 'tx')), may hold values from -0.875 to 0.875
- conv_bias: float32 [256], P(('ty', 'tx')), may hold values from -3 to 3
- neighbour_face: int32 [12, 4], replicated, may hold values from 0 to 11, as said below
- neighbour_side: int32 [12, 4], replicated, may hold values from 0 to 3
- norm_gain: float32 [256], replicated, may hold values from 0.1 to 1.9
- norm_shift: float32 [256], replicated, may hold values from -3 to 3
- expand_weight: bfloat16 [256, 1024], replicated, may hold values from -0.375 to 0.375
- expand_bias: float32 [1024], replicated, may hold values from -3 to 3
- reduce_weight: bfloat16 [1024, 256], replicated, may hold values from -0.1875 to 0.1875
- reduce_bias: float32 [256], replicated, may hold values from -3 to 3
- layer_scale: float32 [256], replicated, may hold values from 0.5 to 1.5
- project_weight: bfloat16 [256, 512], replicated, may hold values from -0.375 to 0.375
- project_bias: float32 [512], replicated, may hold values from -3 to 3
- input_gates: bfloat16 [512, 1536], replicated, may hold values from -0.25 to 0.25
- input_bias: float32 [1536], replicated, may hold values from -3 to 3
- state_gates: bfloat16 [512, 1536], replicated, may hold values from -0.25 to 0.25
- state_bias: float32 [1536], replicated, may hold values from -3 to 3
- hidden_state: float32 [12, 64, 64, 512], P(None, 'ty', 'tx'), may hold values from -6 to 6
Outputs:
- new_state: float32 [12, 64, 64, 512], P(None, 'ty', 'tx')
Inputs may be any that keep to these rules, and one draw needn't show every extreme that they name: Faces are stored in a drawn order. Side s of face f borders side neighbour_side[f, s] of face neighbour_face[f, s], which borders side s of face f back; the 12 faces close into the HEALPix sphere, and positions along two bordering sides run the same way.
All inputs are finite; a program needn't handle non-finite values.
Results may differ from a plain program's by a relative error of at most 0.0032.
Values may be sent and summed in bfloat16 or wider, within the bound.
No kernel may reach another device: no remote copies, remote signals or barrier semaphores. Data moves between devices by JAX's collectives and lax.ppermute only.
A program may use at most 128 MiB of HBM per device.

v0:
```python
import jax
import jax.numpy as jnp
from jax import lax
from jax.experimental import pallas as pl
from jax.experimental.pallas import tpu as pltpu
from jax.sharding import PartitionSpec as P

KERNEL = 7
FACES = 12
SIDE = 128
EPSILON = 1e-06
PADDED = SIDE + 16
DEPTH = (KERNEL + 1) * SIDE

f32 = jnp.float32
bf16 = jnp.bfloat16


def iota(shape, axis):
    return lax.broadcasted_iota(jnp.int32, shape, axis)


def flip_head(tile):
    row = iota(tile.shape, 0)
    return jnp.where(
        row == 7,
        pltpu.roll(tile, 7, 0),
        jnp.where(row == 6, pltpu.roll(tile, 5, 0), pltpu.roll(tile, 3, 0)),
    )


def flip_tail(tile):
    row = iota(tile.shape, 0)
    return jnp.where(
        row == 0,
        pltpu.roll(tile, 1, 0),
        jnp.where(row == 1, pltpu.roll(tile, 3, 0), pltpu.roll(tile, 5, 0)),
    )


def lane_row(shape, axis):
    n = iota(shape, axis)
    return (n & ~15) + ((n & 7) << 1) + ((n >> 3) & 1)


def send_kernel(
    face_ref,
    side_ref,
    kernel_ref,
    bias_ref,
    x_ref,
    msg_ref,
    yt_ref,
    strip_ref,
    flip_ref,
    lhs_ref,
    rhs_ref,
    pool_ref,
    out_ref,
):
    n = lane_row((SIDE, SIDE), 1)
    i = iota((SIDE, SIDE), 0)
    raw = iota((SIDE, SIDE), 1)
    pair = ((i >> 4) == (raw >> 4)) & (((i >> 1) & 7) == (raw & 7))
    for half in range(2):
        pool_ref[half * SIDE : (half + 1) * SIDE, :] = jnp.where(
            pair & (((raw >> 3) & 1) == half), 0.25, 0.0
        ).astype(bf16)

    for c in range(2):

        def prepare(f, carry, c=c):
            x = x_ref[c, f].astype(f32)
            y = x.T
            yt_ref[c, f, 8 : 8 + SIDE, :] = y
            strip_ref[c, f * 4] = x[:8]
            flip_ref[c, f * 4] = flip_head(x[:8])
            strip_ref[c, f * 4 + 1] = flip_tail(x[SIDE - 8 :])
            flip_ref[c, f * 4 + 1] = x[SIDE - 8 :]
            strip_ref[c, f * 4 + 2] = y[:8]
            flip_ref[c, f * 4 + 2] = flip_head(y[:8])
            strip_ref[c, f * 4 + 3] = flip_tail(y[SIDE - 8 :])
            flip_ref[c, f * 4 + 3] = y[SIDE - 8 :]
            return carry

        lax.fori_loop(0, FACES, prepare, 0)

    row8 = iota((8, SIDE), 0)
    lane8 = iota((8, SIDE), 1)
    at_left = (lane8 == SIDE - 1 - row8) & (row8 < 3)
    at_right = (lane8 == row8) & (row8 < 3)

    for c in range(2):
        def weights(value):
            high = value.astype(bf16)
            return high, (value - high.astype(f32)).astype(bf16)

        offset = i - n + 3
        head = lane_row((8, SIDE), 1)
        band = jnp.where(row8 < 4, 2 - row8 - head, SIDE + 3 + (row8 - 4) - head)
        band = jnp.where((row8 & 3) == 3, -1, band)
        borders = []
        for q in range(KERNEL):
            total = jnp.zeros((SIDE, SIDE), f32)
            border = jnp.zeros((8, SIDE), f32)
            for p in range(KERNEL):
                weight = kernel_ref[p * KERNEL + q, c]
                total = jnp.where(offset == p, weight, total)
                border = jnp.where(band == p, weight, border)
            high, low = weights(total)
            rhs_ref[q * SIDE : (q + 1) * SIDE, :SIDE] = high
            rhs_ref[q * SIDE : (q + 1) * SIDE, SIDE:] = low
            borders.append(border)
        borders.append(jnp.zeros((SIDE - 8 * KERNEL, SIDE), f32))
        high, low = weights(jnp.concatenate(borders, axis=0))
        rhs_ref[KERNEL * SIDE :, :SIDE] = high
        rhs_ref[KERNEL * SIDE :, SIDE:] = low

        def assemble(f, carry, c=c):
            at = [face_ref[f, s] * 4 + side_ref[f, s] for s in range(4)]
            left = strip_ref[c, at[2]]
            right = strip_ref[c, at[3]]
            yt_ref[c, f, :8, :] = flip_ref[c, at[2]]
            yt_ref[c, f, 8 + SIDE :, :] = right
            bands = jnp.where(
                row8 < 4, strip_ref[c, at[0]], pltpu.roll(strip_ref[c, at[1]], 4, 0)
            )
            upper = jnp.where(at_left, left[:, :1], 0.0) + jnp.where(at_right, right[:, :1], 0.0)
            lower = jnp.where(at_left, left[:, SIDE - 1 :], 0.0) + jnp.where(
                at_right, right[:, SIDE - 1 :], 0.0
            )
            upper = jnp.sum(upper, axis=0, keepdims=True)
            lower = jnp.sum(lower, axis=0, keepdims=True)
            corner = 0.5 * (
                jnp.where(lane8 >= SIDE // 2, bands[:, :1], bands[:, SIDE - 1 :])
                + jnp.where(row8 < 4, upper, lower)
            )
            shifted = []
            for q in range(KERNEL):
                s = 3 - q
                if s > 0:
                    shifted.append(pltpu.roll(jnp.where(lane8 >= SIDE - s, corner, bands), s, 1))
                elif s < 0:
                    shifted.append(pltpu.roll(jnp.where(lane8 < -s, corner, bands), SIDE + s, 1))
                else:
                    shifted.append(bands)
            shifted.append(jnp.zeros((SIDE - 8 * KERNEL, SIDE), f32))
            rows = pl.ds(pl.multiple_of(f * SIDE, SIDE), SIDE)
            lhs_ref[rows, KERNEL * SIDE :] = jnp.concatenate(shifted, axis=0).T.astype(bf16)
            for q in range(KERNEL):
                lhs_ref[rows, q * SIDE : (q + 1) * SIDE] = yt_ref[
                    c, f, 5 + q : 5 + q + SIDE, :
                ].astype(bf16)
            return carry

        lax.fori_loop(0, FACES, assemble, 0)

        bias = bias_ref[c]
        for part in range(3):
            product = jnp.dot(
                lhs_ref[part * 512 : (part + 1) * 512, :],
                rhs_ref[...],
                preferred_element_type=f32,
            )
            conv = product[:, :SIDE] + product[:, SIDE:] + bias
            for g in range(4):
                f = part * 4 + g
                for t in range(16):
                    at = g * SIDE + t * 8
                    out_ref[t, f * 8 : (f + 1) * 8, :] = conv[at : at + 8]
        middle = slice(3 * SIDE, 4 * SIDE)
        pooled = jnp.dot(
            lhs_ref[: 6 * SIDE, middle], pool_ref[:SIDE, :], preferred_element_type=f32
        ) + jnp.dot(lhs_ref[6 * SIDE :, middle], pool_ref[SIDE:, :], preferred_element_type=f32)
        for f in range(6):
            for t in range(16):
                at = f * SIDE + t * 8
                out_ref[t, 96 + f * 8 : 96 + (f + 1) * 8, :] = pooled[at : at + 8]

        def pack(t, carry, c=c):
            block = jnp.concatenate(
                [
                    out_ref[t, pl.ds(0, 48, stride=2), :],
                    out_ref[t, pl.ds(1, 48, stride=2), :],
                    out_ref[t, pl.ds(96, 24, stride=2), :] + out_ref[t, pl.ds(97, 24, stride=2), :],
                    jnp.zeros((8, SIDE), f32),
                ],
                axis=0,
            )
            block = block.T.astype(bf16)
            for ty in range(8):
                msg_ref[ty, t, c * 16 : (c + 1) * 16, :] = block[ty * 16 : (ty + 1) * 16]
            return carry

        lax.fori_loop(0, 16, pack, 0)


def send(features, conv_kernel, conv_bias, neighbour_face, neighbour_side):
    smem = pl.BlockSpec(memory_space=pltpu.SMEM)
    vmem = pl.BlockSpec(memory_space=pltpu.VMEM)
    return pl.pallas_call(
        send_kernel,
        out_shape=jax.ShapeDtypeStruct((8, 16, 32, SIDE), bf16),
        in_specs=[smem, smem, smem, smem, vmem],
        out_specs=vmem,
        scratch_shapes=[
            pltpu.VMEM((2, FACES, PADDED, SIDE), f32),
            pltpu.VMEM((2, FACES * 4, 8, SIDE), f32),
            pltpu.VMEM((2, FACES * 4, 8, SIDE), f32),
            pltpu.VMEM((FACES * SIDE, DEPTH), bf16),
            pltpu.VMEM((DEPTH, 2 * SIDE), bf16),
            pltpu.VMEM((2 * SIDE, SIDE), bf16),
            pltpu.VMEM((16, 144, SIDE), f32),
        ],
        compiler_params=pltpu.CompilerParams(vmem_limit_bytes=40 * 1024 * 1024),
    )(neighbour_face, neighbour_side, conv_kernel, conv_bias, features)


def receive_kernel(
    msg_ref,
    gain_ref,
    shift_ref,
    expand_ref,
    expand_bias_ref,
    reduce_ref,
    reduce_bias_ref,
    scale_ref,
    project_ref,
    project_bias_ref,
    input_ref,
    input_bias_ref,
    state_ref,
    state_bias_ref,
    hidden_ref,
    out_ref,
    wide_ref,
    normed_ref,
    pooled_ref,
    units_ref,
):
    wide_ref[...] = msg_ref[...].astype(f32)
    lane = iota((256, SIDE), 1)
    gain = gain_ref[...]
    shift = shift_ref[...]
    for r in range(16):
        di, ci = r // 8, r % 8
        values = wide_ref[pl.ds(r, 256, stride=16), :]
        center = jnp.sum(values, axis=0, keepdims=True) * (1.0 / 256)
        away = values - center
        spread = jnp.sum(away * away, axis=0, keepdims=True) * (1.0 / 256)
        scaled = away * lax.rsqrt(spread + EPSILON)
        cells = jnp.where(lane < 96, scaled, values).T
        normed = (cells[:96] * gain + shift).astype(bf16)
        rows = slice(ci * 48, (ci + 1) * 48)
        normed_ref[di * 2, rows, :] = normed[:48]
        normed_ref[di * 2 + 1, rows, :] = normed[48:]
        pooled_ref[ci * 48 + di * 24 : ci * 48 + (di + 1) * 24, :] = cells[96:120]

    for m in range(3):
        rows = slice(m * 128, (m + 1) * 128)
        for k in range(4):
            lanes = slice(k * 256, (k + 1) * 256)
            total = None
            for s in range(4):
                hidden = (
                    jnp.dot(
                        normed_ref[s, rows, :], expand_ref[:, lanes], preferred_element_type=f32
                    )
                    + expand_bias_ref[:, lanes]
                )
                unit = hidden * (1.0 + lax.erf(hidden * (0.5**0.5)))
                total = unit if total is None else total + unit
            units_ref[rows, lanes] = total.astype(bf16)

    update = (
        jnp.dot(units_ref[...], reduce_ref[...], preferred_element_type=f32) * 0.125
        + reduce_bias_ref[...]
    ) * scale_ref[...]
    pooled_ref[...] = pooled_ref[...] + update
    pooled = jnp.concatenate(
        [
            pooled_ref[ci * 48 + f * 4 : ci * 48 + f * 4 + 4, :]
            for f in range(FACES)
            for ci in range(8)
        ],
        axis=0,
    ).astype(bf16)
    mapped = (
        jnp.dot(pooled, project_ref[...], preferred_element_type=f32) + project_bias_ref[...]
    ).astype(bf16)
    for m in range(3):
        rows = slice(m * 128, (m + 1) * 128)
        previous = hidden_ref[rows, :]
        from_input = (
            jnp.dot(mapped[rows], input_ref[...], preferred_element_type=f32) + input_bias_ref[...]
        )
        from_state = (
            jnp.dot(previous.astype(bf16), state_ref[...], preferred_element_type=f32)
            + state_bias_ref[...]
        )
        update_gate = jax.nn.sigmoid(from_input[:, :512] + from_state[:, :512])
        reset_gate = jax.nn.sigmoid(from_input[:, 512:1024] + from_state[:, 512:1024])
        candidate = jnp.tanh(from_input[:, 1024:] + reset_gate * from_state[:, 1024:])
        out_ref[rows, :] = candidate + update_gate * (previous - candidate)


def receive(message, *rest):
    vmem = pl.BlockSpec(memory_space=pltpu.VMEM)
    return pl.pallas_call(
        receive_kernel,
        out_shape=jax.ShapeDtypeStruct((384, 512), f32),
        in_specs=[vmem] * 15,
        out_specs=vmem,
        scratch_shapes=[
            pltpu.VMEM((4096, SIDE), f32),
            pltpu.VMEM((4, 384, 256), bf16),
            pltpu.VMEM((384, 256), f32),
            pltpu.VMEM((384, 1024), bf16),
        ],
        compiler_params=pltpu.CompilerParams(vmem_limit_bytes=48 * 1024 * 1024),
    )(message, *rest)


def shards(
    features,
    conv_kernel,
    conv_bias,
    neighbour_face,
    neighbour_side,
    norm_gain,
    norm_shift,
    expand_weight,
    expand_bias,
    reduce_weight,
    reduce_bias,
    layer_scale,
    project_weight,
    project_bias,
    input_gates,
    input_bias,
    state_gates,
    state_bias,
    hidden_state,
):
    message = send(features, conv_kernel, conv_bias, neighbour_face, neighbour_side)
    message = message.reshape(128, 32, SIDE)
    arrived = lax.all_to_all(message, ("ty", "tx"), split_axis=0, concat_axis=0, tiled=True)
    row = lambda v: v.reshape(1, -1)
    result = receive(
        arrived.reshape(4096, SIDE),
        row(norm_gain),
        row(norm_shift),
        expand_weight,
        row(expand_bias),
        reduce_weight,
        row(reduce_bias),
        row(layer_scale),
        project_weight,
        row(project_bias),
        input_gates,
        row(input_bias),
        state_gates,
        row(state_bias),
        hidden_state.reshape(384, 512),
    )
    return result.reshape(hidden_state.shape)


def solution(mesh):
    placed = (
        P(("ty", "tx"), None, None, None),
        P(None, ("ty", "tx")),
        P(("ty", "tx")),
        P(),
        P(),
        P(),
        P(),
        P(),
        P(),
        P(),
        P(),
        P(),
        P(),
        P(),
        P(),
        P(),
        P(),
        P(),
        P(None, "ty", "tx", None),
    )
    return jax.shard_map(
        shards, mesh=mesh, in_specs=placed, out_specs=P(None, "ty", "tx", None), check_vma=False
    )
```

profile of v0, /device:TPU:1, one launch (start us, length us, event | category | flops | bytes accessed | tf_op | source)
XLA Modules:
  0.0 62.9 jit_solution(5854429138164643638)
XLA Ops:
  0.0 0.8 %copy.22.kernel_ref = f32[49,2]{1,0:T(8,128)S(1)} copy(f32[49,2]{0,1:T(2,128)} %param.20) | data formatting | bytes 784 | tf_op args[1]
  0.8 0.8 %copy.20.face_ref = s32[12,4]{1,0:T(8,128)S(1)} copy(s32[12,4]{0,1:T(4,128)} %param.22) | data formatting | bytes 384 | tf_op args[3]
  1.5 0.8 %copy.21.side_ref = s32[12,4]{1,0:T(8,128)S(1)} copy(s32[12,4]{0,1:T(4,128)} %param.23) | data formatting | bytes 384 | tf_op args[4]
  2.3 1.1 %copy-done.1 = bf16[2,12,128,128]{3,2,1,0:T(8,128)(2,1)S(1)} copy-done((bf16[2,12,128,128]{3,2,1,0:T(8,128)(2,1)S(1)}, bf16[2,12,128,128]{3,2,1,0:T(8,128)(2,1)}, u32[]{:S(2)}) %copy-start.1) | copy-done | bytes 786456
  3.5 0.7 %copy-done.11 = f32[2]{0:T(128)S(1)} copy-done((f32[2]{0:T(128)S(1)}, f32[2]{0:T(128)}, u32[]{:S(2)}) %copy-start.11) | copy-done | bytes 32
  4.1 18.1 %shard_map.181 = bf16[8,16,32,128]{3,2,1,0:T(8,128)(2,1)} custom-call(s32[12,4]{1,0:T(8,128)S(1)} %copy.20.face_ref, s32[12,4]{1,0:T(8,128)S(1)} %copy.21.side_ref, f32[49,2]{1,0:T(8,128)S(1)} %copy.22.kernel_ref, f32[2]{0:T(128)S(1)} %copy-done.11, bf16[2,12,128,128]{3,2,1,0:T(8,128)(2,1)S(1)} %copy-done.1), custom_call_target="tpu_custom_call" | custom-call | tf_op jit(solution)/shard_map/pallas_call | solution.py:201
  22.2 0.0 copy-start.5
  22.2 0.0 copy-start.6
  22.2 0.0 copy-start.7
  22.2 0.0 copy-start.8
  22.3 0.0 copy-start.9
  22.3 0.0 copy-start.10
  22.3 11.5 %all-to-all-start = ((bf16[128,32,128]{2,1,0:T(8,128)(2,1)}), bf16[128,32,128]{2,1,0:T(8,128)(2,1)S(1)}, u32[]{:S(2)}, u32[]{:S(2)}) async-start(bf16[128,32,128]{2,1,0:T(8,128)(2,1)} %bitcast), calls=%async_computation | async-start | bytes 2097152 | tf_op jit(solution)/shard_map/all_to_all | solution.py:347
  33.8 0.0 copy-done.12
  33.8 0.3 reshape.46.hidden_ref
  34.1 0.0 copy-done.13
  34.1 18.7 %all-to-all-done = bf16[128,32,128]{2,1,0:T(8,128)(2,1)S(1)} async-done(((bf16[128,32,128]{2,1,0:T(8,128)(2,1)}), bf16[128,32,128]{2,1,0:T(8,128)(2,1)S(1)}, u32[]{:S(2)}, u32[]{:S(2)}) %all-to-all-start) | async-done | bytes 1048608 | tf_op jit(solution)/shard_map/all_to_all | solution.py:347
  52.9 0.0 copy-done.2
  52.9 0.0 copy-done.5
  52.9 0.0 copy-start
  52.9 1.4 %copy-done = bf16[512,1536]{1,0:T(8,128)(2,1)S(1)} copy-done((bf16[512,1536]{1,0:T(8,128)(2,1)S(1)}, bf16[512,1536]{1,0:T(8,128)(2,1)}, u32[]{:S(2)}) %copy-start) | copy-done | bytes 1572888
  54.3 1.0 %copy-done.3 = bf16[1024,256]{1,0:T(8,128)(2,1)S(1)} copy-done((bf16[1024,256]{1,0:T(8,128)(2,1)S(1)}, bf16[1024,256]{1,0:T(8,128)(2,1)}, u32[]{:S(2)}) %copy-start.3) | copy-done | bytes 524312
  55.4 6.4 %shard_map.182 = f32[384,512]{1,0:T(8,128)S(1)} custom-call(bf16[4096,128]{1,0:T(8,128)(2,1)S(1)} %bitcast.8, f32[1,256]{1,0:T(1,128)S(1)} %bitcast.11, f32[1,256]{1,0:T(1,128)S(1)} %bitcast.12, bf16[256,1024]{1,0:T(8,128)(2,1)S(1)} %copy-done.2, f32[1,1024]{1,0:T(1,128)S(1)} %bitcast.9, bf16[1024,256]{1,0:T(8,128)(2,1)S(1)} %copy-done.3, ...), custom_call_target="tpu_custom_call" | custom-call | tf_op jit(solution)/shard_map/pallas_call | solution.py:309
  61.8 1.1 %reshape.47 = f32[12,8,4,512]{3,2,1,0:T(4,128)} reshape(f32[384,512]{1,0:T(8,128)S(1)} %shard_map.182) | data formatting | bytes 1572864 | tf_op jit(solution)/shard_map/reshape | solution.py:366
  (17 shorter events, 0.0 us)
Async XLA Ops:
  2.3 1.1 %copy-start.1 = (bf16[2,12,128,128]{3,2,1,0:T(8,128)(2,1)S(1)}, bf16[2,12,128,128]{3,2,1,0:T(8,128)(2,1)}, u32[]{:S(2)}) copy-start(bf16[2,12,128,128]{3,2,1,0:T(8,128)(2,1)} %x_ref.1) | copy-start | bytes 2359300
  3.5 0.7 %copy-start.11 = (f32[2]{0:T(128)S(1)}, f32[2]{0:T(128)}, u32[]{:S(2)}) copy-start(f32[2]{0:T(128)} %bias_ref.1) | copy-start | bytes 28
  4.1 29.7 %copy-start.12 = (f32[12,8,4,512]{3,2,1,0:T(4,128)S(1)}, f32[12,8,4,512]{3,2,1,0:T(4,128)}, u32[]{:S(2)}) copy-start(f32[12,8,4,512]{3,2,1,0:T(4,128)} %param.37) | copy-start | bytes 2359300
  22.2 11.9 %copy-start.13 = (f32[1536]{0:T(1024)S(1)}, f32[1536]{0:T(1024)}, u32[]{:S(2)}) copy-start(f32[1536]{0:T(1024)} %param.34) | copy-start | bytes 18436
  22.2 11.9 %copy-start.14 = (f32[1536]{0:T(1024)S(1)}, f32[1536]{0:T(1024)}, u32[]{:S(2)}) copy-start(f32[1536]{0:T(1024)} %param.36) | copy-start | bytes 18436
  22.2 30.7 %copy-start.2 = (bf16[256,1024]{1,0:T(8,128)(2,1)S(1)}, bf16[256,1024]{1,0:T(8,128)(2,1)}, u32[]{:S(2)}) copy-start(bf16[256,1024]{1,0:T(8,128)(2,1)} %expand_ref.1) | copy-start | bytes 1572868
  22.2 30.7 %copy-start.4 = (bf16[256,512]{1,0:T(8,128)(2,1)S(1)}, bf16[256,512]{1,0:T(8,128)(2,1)}, u32[]{:S(2)}) copy-start(bf16[256,512]{1,0:T(8,128)(2,1)} %project_ref.1) | copy-start | bytes 786436
  22.2 30.7 %copy-start.5 = (f32[1024]{0:T(1024)S(1)}, f32[1024]{0:T(1024)}, u32[]{:S(2)}) copy-start(f32[1024]{0:T(1024)} %param.27) | copy-start | bytes 12292
  22.2 30.6 %copy-start.6 = (f32[512]{0:T(512)S(1)}, f32[512]{0:T(512)}, u32[]{:S(2)}) copy-start(f32[512]{0:T(512)} %param.32) | copy-start | bytes 6148
  22.2 30.6 %copy-start.7 = (f32[256]{0:T(256)S(1)}, f32[256]{0:T(256)}, u32[]{:S(2)}) copy-start(f32[256]{0:T(256)} %param.24) | copy-start | bytes 3076
  22.2 30.6 %copy-start.8 = (f32[256]{0:T(256)S(1)}, f32[256]{0:T(256)}, u32[]{:S(2)}) copy-start(f32[256]{0:T(256)} %param.25) | copy-start | bytes 3076
  22.3 30.6 %copy-start.9 = (f32[256]{0:T(256)S(1)}, f32[256]{0:T(256)}, u32[]{:S(2)}) copy-start(f32[256]{0:T(256)} %param.29) | copy-start | bytes 3076
  22.3 30.6 %copy-start.10 = (f32[256]{0:T(256)S(1)}, f32[256]{0:T(256)}, u32[]{:S(2)}) copy-start(f32[256]{0:T(256)} %param.30) | copy-start | bytes 3076
  22.3 30.6 %all-to-all-start = ((bf16[128,32,128]{2,1,0:T(8,128)(2,1)}), bf16[128,32,128]{2,1,0:T(8,128)(2,1)S(1)}, u32[]{:S(2)}, u32[]{:S(2)}) async-start(bf16[128,32,128]{2,1,0:T(8,128)(2,1)} %bitcast), calls=%async_computation | async-start | bytes 2097152 | tf_op jit(solution)/shard_map/all_to_all | solution.py:347
  52.9 1.4 %copy-start = (bf16[512,1536]{1,0:T(8,128)(2,1)S(1)}, bf16[512,1536]{1,0:T(8,128)(2,1)}, u32[]{:S(2)}) copy-start(bf16[512,1536]{1,0:T(8,128)(2,1)} %input_ref.1) | copy-start | bytes 4718596
  54.3 1.0 %copy-start.3 = (bf16[1024,256]{1,0:T(8,128)(2,1)S(1)}, bf16[1024,256]{1,0:T(8,128)(2,1)}, u32[]{:S(2)}) copy-start(bf16[1024,256]{1,0:T(8,128)(2,1)} %reduce_ref.1) | copy-start | bytes 1572868
where the time goes:
time: 63.3 us; the launch traced here: 62.9 us
  Pallas kernels  24.5 us (39%)
  waiting for transfers between devices  18.7 us (30%)
  starting transfers between devices  11.5 us (18%)
  local copies, waits for them, and re-layouts  7.99 us (13%)
    all_to_all x1, waiting for transfers between devices, shards(): lax.all_to_all(message, ('ty', 'tx'), split_axis=0, concat_axis=0, tiled=...  18.7 us
    pallas_call x1, Pallas kernels, send(): pl.pallas_call(send_kernel, out_shape=jax.ShapeDtypeStruct((8, 16, 32, SI...  18.1 us
    all_to_all x1, starting transfers between devices, shards(): lax.all_to_all(message, ('ty', 'tx'), split_axis=0, concat_axis=0, tiled=...  11.5 us
    unnamed x33, local copies, waits for them, and re-layouts  6.6 us
    pallas_call x1, Pallas kernels, receive(): pl.pallas_call(receive_kernel, out_shape=jax.ShapeDtypeStruct((384, 512),...  6.42 us
  transfers between devices with their start and end apart: 1, of which 1 were waited for; matrix products, arithmetic and copies ran while one was open for 0% of the time, Pallas kernels for 0%

commit v1 on v0

--- a/solution.py
+++ b/solution.py
@@ -43,21 +43,7 @@
     return (n & ~15) + ((n & 7) << 1) + ((n >> 3) & 1)
 
 
-def send_kernel(
-    face_ref,
-    side_ref,
-    kernel_ref,
-    bias_ref,
-    x_ref,
-    msg_ref,
-    yt_ref,
-    strip_ref,
-    flip_ref,
-    lhs_ref,
-    rhs_ref,
-    pool_ref,
-    out_ref,
-):
+def weights_kernel(kernel_ref, rhs_ref, pool_ref):
     n = lane_row((SIDE, SIDE), 1)
     i = iota((SIDE, SIDE), 0)
     raw = iota((SIDE, SIDE), 1)
@@ -67,11 +53,54 @@
             pair & (((raw >> 3) & 1) == half), 0.25, 0.0
         ).astype(bf16)
 
+    row8 = iota((8, SIDE), 0)
     for c in range(2):
-
-        def prepare(f, carry, c=c):
-            x = x_ref[c, f].astype(f32)
-            y = x.T
+        def weights(value):
+            high = value.astype(bf16)
+            return high, (value - high.astype(f32)).astype(bf16)
+
+        offset = i - n + 3
+        head = lane_row((8, SIDE), 1)
+        band = jnp.where(row8 < 4, 2 - row8 - head, SIDE + 3 + (row8 - 4) - head)
+        band = jnp.where((row8 & 3) == 3, -1, band)
+        borders = []
+        for q in range(KERNEL):
+            total = jnp.zeros((SIDE, SIDE), f32)
+            border = jnp.zeros((8, SIDE), f32)
+            for p in range(KERNEL):
+                weight = kernel_ref[c, p * KERNEL + q]
+                total = jnp.where(offset == p, weight, total)
+                border = jnp.where(band == p, weight, border)
+            high, low = weights(total)
+            rhs_ref[c, q * SIDE : (q + 1) * SIDE, :SIDE] = high
+            rhs_ref[c, q * SIDE : (q + 1) * SIDE, SIDE:] = low
+            borders.append(border)
+        borders.append(jnp.zeros((SIDE - 8 * KERNEL, SIDE), f32))
+        high, low = weights(jnp.concatenate(borders, axis=0))
+        rhs_ref[c, KERNEL * SIDE :, :SIDE] = high
+        rhs_ref[c, KERNEL * SIDE :, SIDE:] = low
+
+
+def send_kernel(
+    face_ref,
+    side_ref,
+    bias_ref,
+    rhs_ref,
+    pool_ref,
+    x_ref,
+    msg_ref,
+    yt_ref,
+    strip_ref,
+    flip_ref,
+    lhs_ref,
+    out_ref,
+):
+    for c in range(2):
+
+        def prepare(f, c=c):
+            x = x_ref[c, f]
+            y = x.T.astype(f32)
+            x = x.astype(f32)
             yt_ref[c, f, 8 : 8 + SIDE, :] = y
             strip_ref[c, f * 4] = x[:8]
             flip_ref[c, f * 4] = flip_head(x[:8])
@@ -81,9 +110,9 @@
             flip_ref[c, f * 4 + 2] = flip_head(y[:8])
             strip_ref[c, f * 4 + 3] = flip_tail(y[SIDE - 8 :])
             flip_ref[c, f * 4 + 3] = y[SIDE - 8 :]
-            return carry
-
-        lax.fori_loop(0, FACES, prepare, 0)
+
+        for f in range(FACES):
+            prepare(f)
 
     row8 = iota((8, SIDE), 0)
     lane8 = iota((8, SIDE), 1)
@@ -91,33 +120,8 @@
     at_right = (lane8 == row8) & (row8 < 3)
 
     for c in range(2):
-        def weights(value):
-            high = value.astype(bf16)
-            return high, (value - high.astype(f32)).astype(bf16)
-
-        offset = i - n + 3
-        head = lane_row((8, SIDE), 1)
-        band = jnp.where(row8 < 4, 2 - row8 - head, SIDE + 3 + (row8 - 4) - head)
-        band = jnp.where((row8 & 3) == 3, -1, band)
-        borders = []
-        for q in range(KERNEL):
-            total = jnp.zeros((SIDE, SIDE), f32)
-            border = jnp.zeros((8, SIDE), f32)
-            for p in range(KERNEL):
-                weight = kernel_ref[p * KERNEL + q, c]
-                total = jnp.where(offset == p, weight, total)
-                border = jnp.where(band == p, weight, border)
-            high, low = weights(total)
-            rhs_ref[q * SIDE : (q + 1) * SIDE, :SIDE] = high
-            rhs_ref[q * SIDE : (q + 1) * SIDE, SIDE:] = low
-            borders.append(border)
-        borders.append(jnp.zeros((SIDE - 8 * KERNEL, SIDE), f32))
-        high, low = weights(jnp.concatenate(borders, axis=0))
-        rhs_ref[KERNEL * SIDE :, :SIDE] = high
-        rhs_ref[KERNEL * SIDE :, SIDE:] = low
-
-        def assemble(f, carry, c=c):
-            at = [face_ref[f, s] * 4 + side_ref[f, s] for s in range(4)]
+        def assemble(f, c=c):
+            at = [face_ref[s, f] * 4 + side_ref[s, f] for s in range(4)]
             left = strip_ref[c, at[2]]
             right = strip_ref[c, at[3]]
             yt_ref[c, f, :8, :] = flip_ref[c, at[2]]
@@ -145,21 +149,21 @@
                 else:
                     shifted.append(bands)
             shifted.append(jnp.zeros((SIDE - 8 * KERNEL, SIDE), f32))
-            rows = pl.ds(pl.multiple_of(f * SIDE, SIDE), SIDE)
-            lhs_ref[rows, KERNEL * SIDE :] = jnp.concatenate(shifted, axis=0).T.astype(bf16)
+            rows = slice(f * SIDE, (f + 1) * SIDE)
+            lhs_ref[rows, KERNEL * SIDE :] = jnp.concatenate(shifted, axis=0).astype(bf16).T
             for q in range(KERNEL):
                 lhs_ref[rows, q * SIDE : (q + 1) * SIDE] = yt_ref[
                     c, f, 5 + q : 5 + q + SIDE, :
                 ].astype(bf16)
-            return carry
-
-        lax.fori_loop(0, FACES, assemble, 0)
+
+        for f in range(FACES):
+            assemble(f)
 
         bias = bias_ref[c]
         for part in range(3):
             product = jnp.dot(
                 lhs_ref[part * 512 : (part + 1) * 512, :],
-                rhs_ref[...],
+                rhs_ref[c],
                 preferred_element_type=f32,
             )
             conv = product[:, :SIDE] + product[:, SIDE:] + bias
@@ -177,7 +181,7 @@
                 at = f * SIDE + t * 8
                 out_ref[t, 96 + f * 8 : 96 + (f + 1) * 8, :] = pooled[at : at + 8]
 
-        def pack(t, carry, c=c):
+        def pack(t, c=c):
             block = jnp.concatenate(
                 [
                     out_ref[t, pl.ds(0, 48, stride=2), :],
@@ -187,33 +191,45 @@
                 ],
                 axis=0,
             )
-            block = block.T.astype(bf16)
+            block = block.astype(bf16).T
             for ty in range(8):
                 msg_ref[ty, t, c * 16 : (c + 1) * 16, :] = block[ty * 16 : (ty + 1) * 16]
-            return carry
-
-        lax.fori_loop(0, 16, pack, 0)
+
+        for t in range(16):
+            pack(t)
 
 
 def send(features, conv_kernel, conv_bias, neighbour_face, neighbour_side):
     smem = pl.BlockSpec(memory_space=pltpu.SMEM)
     vmem = pl.BlockSpec(memory_space=pltpu.VMEM)
+    rhs, pool = pl.pallas_call(
+        weights_kernel,
+        out_shape=(
+            jax.ShapeDtypeStruct((2, DEPTH, 2 * SIDE), bf16),
+            jax.ShapeDtypeStruct((2 * SIDE, SIDE), bf16),
+        ),
+        in_specs=[smem],
+        out_specs=(vmem, vmem),
+        cost_estimate=pl.CostEstimate(flops=8000000, bytes_accessed=1200000, transcendentals=0),
+        compiler_params=pltpu.CompilerParams(vmem_limit_bytes=4 * 1024 * 1024),
+    )(conv_kernel.T)
     return pl.pallas_call(
         send_kernel,
         out_shape=jax.ShapeDtypeStruct((8, 16, 32, SIDE), bf16),
-        in_specs=[smem, smem, smem, smem, vmem],
+        in_specs=[smem, smem, smem, vmem, vmem, vmem],
         out_specs=vmem,
         scratch_shapes=[
             pltpu.VMEM((2, FACES, PADDED, SIDE), f32),
             pltpu.VMEM((2, FACES * 4, 8, SIDE), f32),
             pltpu.VMEM((2, FACES * 4, 8, SIDE), f32),
             pltpu.VMEM((FACES * SIDE, DEPTH), bf16),
-            pltpu.VMEM((DEPTH, 2 * SIDE), bf16),
-            pltpu.VMEM((2 * SIDE, SIDE), bf16),
             pltpu.VMEM((16, 144, SIDE), f32),
         ],
-        compiler_params=pltpu.CompilerParams(vmem_limit_bytes=40 * 1024 * 1024),
-    )(neighbour_face, neighbour_side, conv_kernel, conv_bias, features)
+        cost_estimate=pl.CostEstimate(
+            flops=2 * 2 * 1536 * DEPTH * 256, bytes_accessed=4000000, transcendentals=0
+        ),
+        compiler_params=pltpu.CompilerParams(vmem_limit_bytes=14 * 1024 * 1024),
+    )(neighbour_face.T, neighbour_side.T, conv_bias, rhs, pool, features)
 
 
 def receive_kernel(
@@ -229,9 +245,8 @@
     project_bias_ref,
     input_ref,
     input_bias_ref,
-    state_ref,
-    state_bias_ref,
-    hidden_ref,
+    previous_ref,
+    from_state_ref,
     out_ref,
     wide_ref,
     normed_ref,
@@ -276,40 +291,63 @@
         jnp.dot(units_ref[...], reduce_ref[...], preferred_element_type=f32) * 0.125
         + reduce_bias_ref[...]
     ) * scale_ref[...]
-    pooled_ref[...] = pooled_ref[...] + update
-    pooled = jnp.concatenate(
-        [
-            pooled_ref[ci * 48 + f * 4 : ci * 48 + f * 4 + 4, :]
-            for f in range(FACES)
-            for ci in range(8)
-        ],
-        axis=0,
-    ).astype(bf16)
+    pooled = (pooled_ref[...] + update).astype(bf16)
     mapped = (
         jnp.dot(pooled, project_ref[...], preferred_element_type=f32) + project_bias_ref[...]
     ).astype(bf16)
-    for m in range(3):
-        rows = slice(m * 128, (m + 1) * 128)
-        previous = hidden_ref[rows, :]
+    for m in range(4):
+        rows = slice(m * 96, (m + 1) * 96)
         from_input = (
             jnp.dot(mapped[rows], input_ref[...], preferred_element_type=f32) + input_bias_ref[...]
         )
-        from_state = (
-            jnp.dot(previous.astype(bf16), state_ref[...], preferred_element_type=f32)
-            + state_bias_ref[...]
+        update_gate = jax.nn.sigmoid(from_input[:, :512] + from_state_ref[rows, :512])
+        reset_gate = jax.nn.sigmoid(from_input[:, 512:1024] + from_state_ref[rows, 512:1024])
+        candidate = jnp.tanh(from_input[:, 1024:] + reset_gate * from_state_ref[rows, 1024:])
+        new = candidate + update_gate * (previous_ref[rows, :] - candidate)
+        for ci in range(2):
+            for f in range(FACES):
+                at = ci * 48 + f * 4
+                out_ref[f, m * 2 + ci] = new[at : at + 4]
+
+
+def state_kernel(hidden_ref, state_ref, bias_ref, previous_ref, from_state_ref):
+    for ci in range(8):
+        for f in range(FACES):
+            at = ci * 48 + f * 4
+            previous_ref[at : at + 4, :] = hidden_ref[f, ci]
+    for m in range(3):
+        rows = slice(m * 128, (m + 1) * 128)
+        from_state_ref[rows, :] = (
+            jnp.dot(
+                previous_ref[rows, :].astype(bf16), state_ref[...], preferred_element_type=f32
+            )
+            + bias_ref[...]
         )
-        update_gate = jax.nn.sigmoid(from_input[:, :512] + from_state[:, :512])
-        reset_gate = jax.nn.sigmoid(from_input[:, 512:1024] + from_state[:, 512:1024])
-        candidate = jnp.tanh(from_input[:, 1024:] + reset_gate * from_state[:, 1024:])
-        out_ref[rows, :] = candidate + update_gate * (previous - candidate)
+
+
+def state_part(hidden, state_gates, state_bias):
+    vmem = pl.BlockSpec(memory_space=pltpu.VMEM)
+    return pl.pallas_call(
+        state_kernel,
+        out_shape=(
+            jax.ShapeDtypeStruct((384, 512), f32),
+            jax.ShapeDtypeStruct((384, 1536), f32),
+        ),
+        in_specs=[vmem] * 3,
+        out_specs=(vmem, vmem),
+        cost_estimate=pl.CostEstimate(
+            flops=2 * 384 * 512 * 1536, bytes_accessed=6000000, transcendentals=0
+        ),
+        compiler_params=pltpu.CompilerParams(vmem_limit_bytes=10 * 1024 * 1024),
+    )(hidden, state_gates, state_bias)
 
 
 def receive(message, *rest):
     vmem = pl.BlockSpec(memory_space=pltpu.VMEM)
     return pl.pallas_call(
         receive_kernel,
-        out_shape=jax.ShapeDtypeStruct((384, 512), f32),
-        in_specs=[vmem] * 15,
+        out_shape=jax.ShapeDtypeStruct((FACES, 8, 4, 512), f32),
+        in_specs=[vmem] * 14,
         out_specs=vmem,
         scratch_shapes=[
             pltpu.VMEM((4096, SIDE), f32),
@@ -317,7 +355,10 @@
             pltpu.VMEM((384, 256), f32),
             pltpu.VMEM((384, 1024), bf16),
         ],
-        compiler_params=pltpu.CompilerParams(vmem_limit_bytes=48 * 1024 * 1024),
+        cost_estimate=pl.CostEstimate(
+            flops=2 * 700000000, bytes_accessed=8000000, transcendentals=2000000
+        ),
+        compiler_params=pltpu.CompilerParams(vmem_limit_bytes=20 * 1024 * 1024),
     )(message, *rest)
 
 
@@ -346,7 +387,8 @@
     message = message.reshape(128, 32, SIDE)
     arrived = lax.all_to_all(message, ("ty", "tx"), split_axis=0, concat_axis=0, tiled=True)
     row = lambda v: v.reshape(1, -1)
-    result = receive(
+    previous, from_state = state_part(hidden_state, state_gates, row(state_bias))
+    return receive(
         arrived.reshape(4096, SIDE),
         row(norm_gain),
         row(norm_shift),
@@ -359,11 +401,9 @@
         row(project_bias),
         input_gates,
         row(input_bias),
-        state_gates,
-        row(state_bias),
-        hidden_state.reshape(384, 512),
+        previous,
+        from_state,
     )
-    return result.reshape(hidden_state.shape)
 
 
 def solution(mesh):

time: 63.3 us -> 51.9 us (0.82)
  Pallas kernels: 24.5 us -> 12.1 us
  local copies, waits for them, and re-layouts: 7.99 us -> 12.9 us
  waiting for transfers between devices: 18.7 us -> 14.7 us
    pallas_call x1, Pallas kernels: 18.1 us -> 4.71 us  [send(): pl.pallas_call(send_kernel, out_shape=jax.ShapeDtypeStruct((8, 16, 32, SI...]
    unnamed x33 -> x42, local copies, waits for them, and re-layouts: 6.6 us -> 12.8 us
    all_to_all x1, waiting for transfers between devices: 18.7 us -> 14.7 us  [shards(): lax.all_to_all(message, ('ty', 'tx'), split_axis=0, concat_axis=0, tiled=...]
    reshape x2 -> x0, local copies, waits for them, and re-layouts: 1.38 us -> none  [the longest x1 1.11 us: shards(): return result.reshape(hidden_state.shape)]
    pallas_call x1 -> x3, Pallas kernels: 6.42 us -> 7.42 us  [the longest x1 5.41 us: receive(): pl.pallas_call(receive_kernel, out_shape=jax.ShapeDtypeStruct((FACES, 8,...]
  transfers between devices with their start and end apart: 1 -> 1, of which waited for: 1 -> 1; matrix products, arithmetic and copies ran while one was open for 0% -> 0% of each run, Pallas kernels for 0% -> 2%
where the time goes in v1:
time: 51.9 us; the launch traced here: 51.4 us
  waiting for transfers between devices  14.7 us (28%)
  local copies, waits for them, and re-layouts  12.9 us (25%)
  Pallas kernels  12.1 us (23%)
  starting transfers between devices  11.5 us (22%)
    all_to_all x1, waiting for transfers between devices, shards(): lax.all_to_all(message, ('ty', 'tx'), split_axis=0, concat_axis=0, tiled=...  14.7 us
    unnamed x42, local copies, waits for them, and re-layouts  12.8 us
    all_to_all x1, starting transfers between devices, shards(): lax.all_to_all(message, ('ty', 'tx'), split_axis=0, concat_axis=0, tiled=...  11.5 us
    pallas_call x1, Pallas kernels, receive(): pl.pallas_call(receive_kernel, out_shape=jax.ShapeDtypeStruct((FACES, 8,...  5.41 us
    pallas_call x1, Pallas kernels, send(): pl.pallas_call(send_kernel, out_shape=jax.ShapeDtypeStruct((8, 16, 32, SI...  4.71 us
    pallas_call x1, Pallas kernels, send(): pl.pallas_call(weights_kernel, out_shape=(jax.ShapeDtypeStruct((2, DEPTH,...  1.2 us
  transfers between devices with their start and end apart: 1, of which 1 were waited for; matrix products, arithmetic and copies ran while one was open for 0% of the time, Pallas kernels for 2%

profile of v1, /device:TPU:1, one launch (start us, length us, event | category | flops | bytes accessed | tf_op | source)
XLA Modules:
  0.0 51.4 jit_solution(3543483919355498624)
XLA Ops:
  0.0 0.7 %copy-done.17 = f32[49,2]{0,1:T(2,128)S(1)} copy-done((f32[49,2]{0,1:T(2,128)S(1)}, f32[49,2]{0,1:T(2,128)}, u32[]{:S(2)}) %copy-start.17) | copy-done | bytes 416
  0.7 1.2 %shard_map.181 = (bf16[2,1024,256]{2,1,0:T(8,128)(2,1)S(1)}, bf16[256,128]{1,0:T(8,128)(2,1)S(1)}) custom-call(f32[2,49]{1,0:T(2,128)S(1)} %bitcast.20), custom_call_target="tpu_custom_call" | custom-call | flops 8000000 | bytes 1200000 | tf_op jit(solution)/shard_map/pallas_call | solution.py:205
  1.9 0.0 copy-start.14
  1.9 1.1 %copy-done.14 = bf16[2,12,128,128]{3,2,1,0:T(8,128)(2,1)S(1)} copy-done((bf16[2,12,128,128]{3,2,1,0:T(8,128)(2,1)S(1)}, bf16[2,12,128,128]{3,2,1,0:T(8,128)(2,1)}, u32[]{:S(2)}) %copy-start.14) | copy-done | bytes 786456
  3.0 0.7 %copy-done.15 = s32[12,4]{0,1:T(4,128)S(1)} copy-done((s32[12,4]{0,1:T(4,128)S(1)}, s32[12,4]{0,1:T(4,128)}, u32[]{:S(2)}) %copy-start.15) | copy-done | bytes 216
  3.7 0.7 %copy-done.16 = s32[12,4]{0,1:T(4,128)S(1)} copy-done((s32[12,4]{0,1:T(4,128)S(1)}, s32[12,4]{0,1:T(4,128)}, u32[]{:S(2)}) %copy-start.16) | copy-done | bytes 216
  4.4 0.7 %copy-done.18 = f32[2]{0:T(128)S(1)} copy-done((f32[2]{0:T(128)S(1)}, f32[2]{0:T(128)}, u32[]{:S(2)}) %copy-start.18) | copy-done | bytes 32
  5.0 4.7 %shard_map.182 = bf16[8,16,32,128]{3,2,1,0:T(8,128)(2,1)} custom-call(s32[4,12]{1,0:T(4,128)S(1)} %bitcast.18, s32[4,12]{1,0:T(4,128)S(1)} %bitcast.19, f32[2]{0:T(128)S(1)} %copy-done.18, bf16[2,1024,256]{2,1,0:T(8,128)(2,1)S(1)} %get-tuple-element.9.rhs_ref, bf16[256,128]{1,0:T(8,128)(2,1)S(1)} %get-tuple-element.10.pool_ref, ...), custom_call_target="tpu_custom_call" | custom-call | flops 1610612736 | bytes 4000000 | tf_op jit(solution)/shard_map/pallas_call | solution.py:216
  9.8 11.5 %all-to-all-start = ((bf16[128,32,128]{2,1,0:T(8,128)(2,1)}), bf16[128,32,128]{2,1,0:T(8,128)(2,1)S(1)}, u32[]{:S(2)}, u32[]{:S(2)}) async-start(bf16[128,32,128]{2,1,0:T(8,128)(2,1)} %bitcast.3), calls=%async_computation | async-start | bytes 2097152 | tf_op jit(solution)/shard_map/all_to_all | solution.py:388
  21.3 0.0 copy-start.8
  21.3 0.0 copy-start.10
  21.3 0.0 copy-start.11
  21.4 0.0 copy-start
  21.4 1.4 %copy-done = bf16[512,1536]{1,0:T(8,128)(2,1)S(1)} copy-done((bf16[512,1536]{1,0:T(8,128)(2,1)S(1)}, bf16[512,1536]{1,0:T(8,128)(2,1)}, u32[]{:S(2)}) %copy-start) | copy-done | bytes 1572888
  22.8 1.1 %copy-done.2 = f32[12,8,4,512]{3,2,1,0:T(4,128)S(1)} copy-done((f32[12,8,4,512]{3,2,1,0:T(4,128)S(1)}, f32[12,8,4,512]{3,2,1,0:T(4,128)}, u32[]{:S(2)}) %copy-start.2) | copy-done | bytes 786456
  23.9 0.8 %shard_map.183 = (f32[384,512]{1,0:T(8,128)S(1)}, f32[384,1536]{1,0:T(8,128)S(1)}) custom-call(f32[12,8,4,512]{3,2,1,0:T(4,128)S(1)} %copy-done.2, bf16[512,1536]{1,0:T(8,128)(2,1)S(1)} %copy-done, f32[1,1536]{1,0:T(1,128)S(1)} %reshape.39.bias_ref), custom_call_target="tpu_custom_call" | custom-call | flops 603979776 | bytes 6000000 | tf_op jit(solution)/shard_map/pallas_call | solution.py:330
  24.7 0.9 %copy-done.3 = f32[384,512]{1,0:T(8,128)} copy-done((f32[384,512]{1,0:T(8,128)}, f32[384,512]{1,0:T(8,128)S(1)}, u32[]{:S(2)}) %copy-start.3) | copy-done | bytes 786456
  25.6 14.7 %all-to-all-done = bf16[128,32,128]{2,1,0:T(8,128)(2,1)S(1)} async-done(((bf16[128,32,128]{2,1,0:T(8,128)(2,1)}), bf16[128,32,128]{2,1,0:T(8,128)(2,1)S(1)}, u32[]{:S(2)}, u32[]{:S(2)}) %all-to-all-start) | async-done | bytes 1048608 | tf_op jit(solution)/shard_map/all_to_all | solution.py:388
  40.4 1.4 %copy-done.1 = bf16[512,1536]{1,0:T(8,128)(2,1)S(1)} copy-done((bf16[512,1536]{1,0:T(8,128)(2,1)S(1)}, bf16[512,1536]{1,0:T(8,128)(2,1)}, u32[]{:S(2)}) %copy-start.1) | copy-done | bytes 1572888
  41.8 1.1 %copy-done.4 = f32[384,512]{1,0:T(8,128)S(1)} copy-done((f32[384,512]{1,0:T(8,128)S(1)}, f32[384,512]{1,0:T(8,128)}, u32[]{:S(2)}) %copy-start.4) | copy-done | bytes 786456
  42.9 1.0 %copy-done.5 = bf16[256,1024]{1,0:T(8,128)(2,1)S(1)} copy-done((bf16[256,1024]{1,0:T(8,128)(2,1)S(1)}, bf16[256,1024]{1,0:T(8,128)(2,1)}, u32[]{:S(2)}) %copy-start.5) | copy-done | bytes 524312
  44.0 1.0 %copy-done.6 = bf16[1024,256]{1,0:T(8,128)(2,1)S(1)} copy-done((bf16[1024,256]{1,0:T(8,128)(2,1)S(1)}, bf16[1024,256]{1,0:T(8,128)(2,1)}, u32[]{:S(2)}) %copy-start.6) | copy-done | bytes 524312
  45.0 0.9 %copy-done.7 = bf16[256,512]{1,0:T(8,128)(2,1)S(1)} copy-done((bf16[256,512]{1,0:T(8,128)(2,1)S(1)}, bf16[256,512]{1,0:T(8,128)(2,1)}, u32[]{:S(2)}) %copy-start.7) | copy-done | bytes 262168
  45.9 5.4 %shard_map.184 = f32[12,8,4,512]{3,2,1,0:T(4,128)} custom-call(bf16[4096,128]{1,0:T(8,128)(2,1)S(1)} %bitcast.11, f32[1,256]{1,0:T(1,128)S(1)} %bitcast.14, f32[1,256]{1,0:T(1,128)S(1)} %bitcast.15, bf16[256,1024]{1,0:T(8,128)(2,1)S(1)} %copy-done.5, f32[1,1024]{1,0:T(1,128)S(1)} %bitcast.12, bf16[1024,256]{1,0:T(8,128)(2,1)S(1)} %copy-done.6, ...), custom_call_target="tpu_custom_call" | custom-call | flops 1400000000 | bytes 8000000 | tf_op jit(solution)/shard_map/pallas_call | solution.py:347
  (26 shorter events, 0.1 us)
Async XLA Ops:
  0.0 0.7 %copy-start.17 = (f32[49,2]{0,1:T(2,128)S(1)}, f32[49,2]{0,1:T(2,128)}, u32[]{:S(2)}) copy-start(f32[49,2]{0,1:T(2,128)} %param.20) | copy-start | bytes 1180
  1.9 1.1 %copy-start.14 = (bf16[2,12,128,128]{3,2,1,0:T(8,128)(2,1)S(1)}, bf16[2,12,128,128]{3,2,1,0:T(8,128)(2,1)}, u32[]{:S(2)}) copy-start(bf16[2,12,128,128]{3,2,1,0:T(8,128)(2,1)} %x_ref.1) | copy-start | bytes 2359300
  3.0 0.7 %copy-start.15 = (s32[12,4]{0,1:T(4,128)S(1)}, s32[12,4]{0,1:T(4,128)}, u32[]{:S(2)}) copy-start(s32[12,4]{0,1:T(4,128)} %param.22) | copy-start | bytes 580
  3.7 0.7 %copy-start.16 = (s32[12,4]{0,1:T(4,128)S(1)}, s32[12,4]{0,1:T(4,128)}, u32[]{:S(2)}) copy-start(s32[12,4]{0,1:T(4,128)} %param.23) | copy-start | bytes 580
  4.4 0.7 %copy-start.18 = (f32[2]{0:T(128)S(1)}, f32[2]{0:T(128)}, u32[]{:S(2)}) copy-start(f32[2]{0:T(128)} %bias_ref.1) | copy-start | bytes 28
  9.8 11.5 %copy-start.19 = (f32[1536]{0:T(1024)S(1)}, f32[1536]{0:T(1024)}, u32[]{:S(2)}) copy-start(f32[1536]{0:T(1024)} %param.34) | copy-start | bytes 18436
  9.8 11.6 %copy-start.20 = (f32[1536]{0:T(1024)S(1)}, f32[1536]{0:T(1024)}, u32[]{:S(2)}) copy-start(f32[1536]{0:T(1024)} %param.36) | copy-start | bytes 18436
  9.8 30.6 %all-to-all-start = ((bf16[128,32,128]{2,1,0:T(8,128)(2,1)}), bf16[128,32,128]{2,1,0:T(8,128)(2,1)S(1)}, u32[]{:S(2)}, u32[]{:S(2)}) async-start(bf16[128,32,128]{2,1,0:T(8,128)(2,1)} %bitcast.3), calls=%async_computation | async-start | bytes 2097152 | tf_op jit(solution)/shard_map/all_to_all | solution.py:388
  21.3 19.1 %copy-start.8 = (f32[1024]{0:T(1024)S(1)}, f32[1024]{0:T(1024)}, u32[]{:S(2)}) copy-start(f32[1024]{0:T(1024)} %param.27) | copy-start | bytes 12292
  21.3 19.0 %copy-start.9 = (f32[512]{0:T(512)S(1)}, f32[512]{0:T(512)}, u32[]{:S(2)}) copy-start(f32[512]{0:T(512)} %param.32) | copy-start | bytes 6148
  21.3 19.0 %copy-start.10 = (f32[256]{0:T(256)S(1)}, f32[256]{0:T(256)}, u32[]{:S(2)}) copy-start(f32[256]{0:T(256)} %param.24) | copy-start | bytes 3076
  21.3 19.0 %copy-start.11 = (f32[256]{0:T(256)S(1)}, f32[256]{0:T(256)}, u32[]{:S(2)}) copy-start(f32[256]{0:T(256)} %param.25) | copy-start | bytes 3076
  21.3 19.0 %copy-start.12 = (f32[256]{0:T(256)S(1)}, f32[256]{0:T(256)}, u32[]{:S(2)}) copy-start(f32[256]{0:T(256)} %param.29) | copy-start | bytes 3076
  21.3 19.0 %copy-start.13 = (f32[256]{0:T(256)S(1)}, f32[256]{0:T(256)}, u32[]{:S(2)}) copy-start(f32[256]{0:T(256)} %param.30) | copy-start | bytes 3076
  21.4 1.4 %copy-start = (bf16[512,1536]{1,0:T(8,128)(2,1)S(1)}, bf16[512,1536]{1,0:T(8,128)(2,1)}, u32[]{:S(2)}) copy-start(bf16[512,1536]{1,0:T(8,128)(2,1)} %state_ref.1) | copy-start | bytes 4718596
  22.8 1.1 %copy-start.2 = (f32[12,8,4,512]{3,2,1,0:T(4,128)S(1)}, f32[12,8,4,512]{3,2,1,0:T(4,128)}, u32[]{:S(2)}) copy-start(f32[12,8,4,512]{3,2,1,0:T(4,128)} %hidden_ref.1) | copy-start | bytes 2359300
  24.7 0.9 %copy-start.3 = (f32[384,512]{1,0:T(8,128)}, f32[384,512]{1,0:T(8,128)S(1)}, u32[]{:S(2)}) copy-start(f32[384,512]{1,0:T(8,128)S(1)} %get-tuple-element.11.previous_ref) | copy-start | bytes 2359300
  40.4 1.4 %copy-start.1 = (bf16[512,1536]{1,0:T(8,128)(2,1)S(1)}, bf16[512,1536]{1,0:T(8,128)(2,1)}, u32[]{:S(2)}) copy-start(bf16[512,1536]{1,0:T(8,128)(2,1)} %input_ref.1) | copy-start | bytes 4718596
  41.8 1.1 %copy-start.4 = (f32[384,512]{1,0:T(8,128)S(1)}, f32[384,512]{1,0:T(8,128)}, u32[]{:S(2)}) copy-start(f32[384,512]{1,0:T(8,128)} %copy-done.3) | copy-start | bytes 2359300
  42.9 1.0 %copy-start.5 = (bf16[256,1024]{1,0:T(8,128)(2,1)S(1)}, bf16[256,1024]{1,0:T(8,128)(2,1)}, u32[]{:S(2)}) copy-start(bf16[256,1024]{1,0:T(8,128)(2,1)} %expand_ref.1) | copy-start | bytes 1572868
  44.0 1.0 %copy-start.6 = (bf16[1024,256]{1,0:T(8,128)(2,1)S(1)}, bf16[1024,256]{1,0:T(8,128)(2,1)}, u32[]{:S(2)}) copy-start(bf16[1024,256]{1,0:T(8,128)(2,1)} %reduce_ref.1) | copy-start | bytes 1572868
  45.0 0.9 %copy-start.7 = (bf16[256,512]{1,0:T(8,128)(2,1)S(1)}, bf16[256,512]{1,0:T(8,128)(2,1)}, u32[]{:S(2)}) copy-start(bf16[256,512]{1,0:T(8,128)(2,1)} %project_ref.1) | copy-start | bytes 786436

commit v2 on v1

--- a/solution.py
+++ b/solution.py
@@ -11,6 +11,8 @@
 EPSILON = 1e-06
 PADDED = SIDE + 16
 DEPTH = (KERNEL + 1) * SIDE
+
+SEND_VMEM = 63 * 1024 * 1024
 
 f32 = jnp.float32
 bf16 = jnp.bfloat16
@@ -43,8 +45,44 @@
     return (n & ~15) + ((n & 7) << 1) + ((n >> 3) & 1)
 
 
-def weights_kernel(kernel_ref, rhs_ref, pool_ref):
-    n = lane_row((SIDE, SIDE), 1)
+def send_kernel(
+    kernel_hbm,
+    face_hbm,
+    side_hbm,
+    bias_hbm,
+    x_hbm,
+    msg_hbm,
+    kernel_ref,
+    face_ref,
+    side_ref,
+    bias_ref,
+    x_ref,
+    yt_ref,
+    strip_ref,
+    flip_ref,
+    lhs_ref,
+    rhs_ref,
+    pool_ref,
+    out_ref,
+    msg_ref,
+    small_sem,
+    x_sem,
+    msg_sem,
+):
+    loads = [
+        pltpu.make_async_copy(source, target, small_sem.at[k])
+        for k, (source, target) in enumerate(
+            [
+                (kernel_hbm, kernel_ref),
+                (face_hbm, face_ref),
+                (side_hbm, side_ref),
+                (bias_hbm, bias_ref),
+            ]
+        )
+    ] + [pltpu.make_async_copy(x_hbm.at[c], x_ref.at[c], x_sem.at[c]) for c in range(2)]
+    for copy in loads:
+        copy.start()
+
     i = iota((SIDE, SIDE), 0)
     raw = iota((SIDE, SIDE), 1)
     pair = ((i >> 4) == (raw >> 4)) & (((i >> 1) & 7) == (raw & 7))
@@ -54,47 +92,44 @@
         ).astype(bf16)
 
     row8 = iota((8, SIDE), 0)
+    lane8 = iota((8, SIDE), 1)
+    at_left = (lane8 == SIDE - 1 - row8) & (row8 < 3)
+    at_right = (lane8 == row8) & (row8 < 3)
+    lane16 = iota((16, SIDE), 1)
+    offset = 64 + iota((16, SIDE), 0) - lane_row((16, SIDE), 1) + 3
+    head = lane_row((8, SIDE), 1)
+    band = jnp.where(row8 < 4, 2 - row8 - head, SIDE + 3 + (row8 - 4) - head)
+    band = jnp.where((row8 & 3) == 3, -1, band)
+
+    for copy in loads:
+        copy.wait()
+
+    def store_weights(c, rows, value):
+        high = value.astype(bf16)
+        rhs_ref[c, rows, :SIDE] = high
+        rhs_ref[c, rows, SIDE:] = (value - high.astype(f32)).astype(bf16)
+
     for c in range(2):
-        def weights(value):
-            high = value.astype(bf16)
-            return high, (value - high.astype(f32)).astype(bf16)
-
-        offset = i - n + 3
-        head = lane_row((8, SIDE), 1)
-        band = jnp.where(row8 < 4, 2 - row8 - head, SIDE + 3 + (row8 - 4) - head)
-        band = jnp.where((row8 & 3) == 3, -1, band)
         borders = []
         for q in range(KERNEL):
-            total = jnp.zeros((SIDE, SIDE), f32)
+            base = jnp.zeros((16, SIDE), f32)
             border = jnp.zeros((8, SIDE), f32)
             for p in range(KERNEL):
                 weight = kernel_ref[c, p * KERNEL + q]
-                total = jnp.where(offset == p, weight, total)
+                base = jnp.where(offset == p, weight, base)
                 border = jnp.where(band == p, weight, border)
-            high, low = weights(total)
-            rhs_ref[c, q * SIDE : (q + 1) * SIDE, :SIDE] = high
-            rhs_ref[c, q * SIDE : (q + 1) * SIDE, SIDE:] = low
+            for k in range(8):
+                value = base if k == 4 else pltpu.roll(base, (16 * (k - 4)) % SIDE, 1)
+                if k == 0:
+                    value = jnp.where(lane16 >= SIDE - 16, 0.0, value)
+                if k == 7:
+                    value = jnp.where(lane16 < 16, 0.0, value)
+                at = q * SIDE + k * 16
+                store_weights(c, slice(at, at + 16), value)
             borders.append(border)
         borders.append(jnp.zeros((SIDE - 8 * KERNEL, SIDE), f32))
-        high, low = weights(jnp.concatenate(borders, axis=0))
-        rhs_ref[c, KERNEL * SIDE :, :SIDE] = high
-        rhs_ref[c, KERNEL * SIDE :, SIDE:] = low
-
-
-def send_kernel(
-    face_ref,
-    side_ref,
-    bias_ref,
-    rhs_ref,
-    pool_ref,
-    x_ref,
-    msg_ref,
-    yt_ref,
-    strip_ref,
-    flip_ref,
-    lhs_ref,
-    out_ref,
-):
+        store_weights(c, slice(KERNEL * SIDE, DEPTH), jnp.concatenate(borders, axis=0))
+
     for c in range(2):
 
         def prepare(f, c=c):
@@ -114,12 +149,9 @@
         for f in range(FACES):
             prepare(f)
 
-    row8 = iota((8, SIDE), 0)
-    lane8 = iota((8, SIDE), 1)
-    at_left = (lane8 == SIDE - 1 - row8) & (row8 < 3)
-    at_right = (lane8 == row8) & (row8 < 3)
-
+    sends = []
     for c in range(2):
+
         def assemble(f, c=c):
             at = [face_ref[s, f] * 4 + side_ref[s, f] for s in range(4)]
             left = strip_ref[c, at[2]]
@@ -197,39 +229,48 @@
 
         for t in range(16):
             pack(t)
+        sends.append(
+            pltpu.make_async_copy(
+                msg_ref.at[:, :, pl.ds(c * 16, 16)],
+                msg_hbm.at[:, :, pl.ds(c * 16, 16)],
+                msg_sem.at[c],
+            )
+        )
+        sends[-1].start()
+    for copy in sends:
+        copy.wait()
 
 
 def send(features, conv_kernel, conv_bias, neighbour_face, neighbour_side):
-    smem = pl.BlockSpec(memory_space=pltpu.SMEM)
-    vmem = pl.BlockSpec(memory_space=pltpu.VMEM)
-    rhs, pool = pl.pallas_call(
-        weights_kernel,
-        out_shape=(
-            jax.ShapeDtypeStruct((2, DEPTH, 2 * SIDE), bf16),
-            jax.ShapeDtypeStruct((2 * SIDE, SIDE), bf16),
-        ),
-        in_specs=[smem],
-        out_specs=(vmem, vmem),
-        cost_estimate=pl.CostEstimate(flops=8000000, bytes_accessed=1200000, transcendentals=0),
-        compiler_params=pltpu.CompilerParams(vmem_limit_bytes=4 * 1024 * 1024),
-    )(conv_kernel.T)
+    hbm = pl.BlockSpec(memory_space=pl.ANY)
     return pl.pallas_call(
         send_kernel,
         out_shape=jax.ShapeDtypeStruct((8, 16, 32, SIDE), bf16),
-        in_specs=[smem, smem, smem, vmem, vmem, vmem],
-        out_specs=vmem,
+        in_specs=[hbm] * 5,
+        out_specs=hbm,
         scratch_shapes=[
+            pltpu.SMEM((2, KERNEL * KERNEL), f32),
+            pltpu.SMEM((4, FACES), jnp.int32),
+            pltpu.SMEM((4, FACES), jnp.int32),
+            pltpu.SMEM((2,), f32),
+            pltpu.VMEM((2, FACES, SIDE, SIDE), bf16),
             pltpu.VMEM((2, FACES, PADDED, SIDE), f32),
             pltpu.VMEM((2, FACES * 4, 8, SIDE), f32),
             pltpu.VMEM((2, FACES * 4, 8, SIDE), f32),
             pltpu.VMEM((FACES * SIDE, DEPTH), bf16),
+            pltpu.VMEM((2, DEPTH, 2 * SIDE), bf16),
+            pltpu.VMEM((2 * SIDE, SIDE), bf16),
             pltpu.VMEM((16, 144, SIDE), f32),
+            pltpu.VMEM((8, 16, 32, SIDE), bf16),
+            pltpu.SemaphoreType.DMA((4,)),
+            pltpu.SemaphoreType.DMA((2,)),
+            pltpu.SemaphoreType.DMA((2,)),
         ],
         cost_estimate=pl.CostEstimate(
             flops=2 * 2 * 1536 * DEPTH * 256, bytes_accessed=4000000, transcendentals=0
         ),
-        compiler_params=pltpu.CompilerParams(vmem_limit_bytes=14 * 1024 * 1024),
-    )(neighbour_face.T, neighbour_side.T, conv_bias, rhs, pool, features)
+        compiler_params=pltpu.CompilerParams(vmem_limit_bytes=SEND_VMEM),
+    )(conv_kernel.T, neighbour_face.T, neighbour_side.T, conv_bias, features)
 
 
 def receive_kernel(
@@ -263,27 +304,26 @@
         center = jnp.sum(values, axis=0, keepdims=True) * (1.0 / 256)
         away = values - center
         spread = jnp.sum(away * away, axis=0, keepdims=True) * (1.0 / 256)
-        scaled = away * lax.rsqrt(spread + EPSILON)
-        cells = jnp.where(lane < 96, scaled, values).T
-        normed = (cells[:96] * gain + shift).astype(bf16)
+        normed = away * lax.rsqrt(spread + EPSILON) * gain + shift
+        cells = jnp.where(lane < 96, normed, values).astype(bf16).T
         rows = slice(ci * 48, (ci + 1) * 48)
-        normed_ref[di * 2, rows, :] = normed[:48]
-        normed_ref[di * 2 + 1, rows, :] = normed[48:]
-        pooled_ref[ci * 48 + di * 24 : ci * 48 + (di + 1) * 24, :] = cells[96:120]
-
-    for m in range(3):
-        rows = slice(m * 128, (m + 1) * 128)
-        for k in range(4):
-            lanes = slice(k * 256, (k + 1) * 256)
+        normed_ref[di * 2, rows, :] = cells[:48]
+        normed_ref[di * 2 + 1, rows, :] = cells[48:96]
+        pooled_ref[ci * 48 + di * 24 : ci * 48 + (di + 1) * 24, :] = cells[96:].astype(f32)[:24]
+
+    for k in range(4):
+        lanes = slice(k * 256, (k + 1) * 256)
+        for m in range(3):
+            rows = slice(m * 128, (m + 1) * 128)
+            hidden = jnp.dot(
+                normed_ref[:, rows, :].reshape(512, 256),
+                expand_ref[:, lanes],
+                preferred_element_type=f32,
+            )
             total = None
             for s in range(4):
-                hidden = (
-                    jnp.dot(
-                        normed_ref[s, rows, :], expand_ref[:, lanes], preferred_element_type=f32
-                    )
-                    + expand_bias_ref[:, lanes]
-                )
-                unit = hidden * (1.0 + lax.erf(hidden * (0.5**0.5)))
+                part = hidden[s * 128 : (s + 1) * 128] + expand_bias_ref[:, lanes]
+                unit = part * (1.0 + lax.erf(part * (0.5**0.5)))
                 total = unit if total is None else total + unit
             units_ref[rows, lanes] = total.astype(bf16)
 
@@ -295,54 +335,94 @@
     mapped = (
         jnp.dot(pooled, project_ref[...], preferred_element_type=f32) + project_bias_ref[...]
     ).astype(bf16)
-    for m in range(4):
-        rows = slice(m * 96, (m + 1) * 96)
-        from_input = (
-            jnp.dot(mapped[rows], input_ref[...], preferred_element_type=f32) + input_bias_ref[...]
-        )
-        update_gate = jax.nn.sigmoid(from_input[:, :512] + from_state_ref[rows, :512])
-        reset_gate = jax.nn.sigmoid(from_input[:, 512:1024] + from_state_ref[rows, 512:1024])
-        candidate = jnp.tanh(from_input[:, 1024:] + reset_gate * from_state_ref[rows, 1024:])
-        new = candidate + update_gate * (previous_ref[rows, :] - candidate)
-        for ci in range(2):
+
+    def sigmoid(v):
+        return 0.5 * jnp.tanh(0.5 * v) + 0.5
+
+    for k in range(2):
+
+        def gate(block):
+            lanes = slice(block * 512 + k * 256, block * 512 + (k + 1) * 256)
+            return (
+                jnp.dot(mapped, input_ref[:, lanes], preferred_element_type=f32)
+                + input_bias_ref[:, lanes],
+                from_state_ref[:, lanes],
+            )
+
+        lanes = slice(k * 256, (k + 1) * 256)
+        a, b = gate(0)
+        update_gate = sigmoid(a + b)
+        a, b = gate(1)
+        reset_gate = sigmoid(a + b)
+        a, b = gate(2)
+        candidate = jnp.tanh(a + reset_gate * b)
+        new = candidate + update_gate * (previous_ref[:, lanes] - candidate)
+        for ci in range(8):
             for f in range(FACES):
                 at = ci * 48 + f * 4
-                out_ref[f, m * 2 + ci] = new[at : at + 4]
-
-
-def state_kernel(hidden_ref, state_ref, bias_ref, previous_ref, from_state_ref):
+                out_ref[f, ci, :, lanes] = new[at : at + 4]
+
+
+def ready_kernel(*refs):
+    hidden_ref, state_ref, state_bias_ref, gain_ref, shift_ref = refs[:5]
+    vectors, matrices = refs[5:10], refs[10:14]
+    previous_ref, from_state_ref, gain_out, shift_out = refs[14:18]
+    vectors_out, matrices_out = refs[18:23], refs[23:27]
+    sems = refs[27]
+    copies = [
+        pltpu.make_async_copy(source, target, sems.at[k])
+        for k, (source, target) in enumerate(zip(matrices, matrices_out))
+    ]
+    for copy in copies:
+        copy.start()
     for ci in range(8):
         for f in range(FACES):
             at = ci * 48 + f * 4
             previous_ref[at : at + 4, :] = hidden_ref[f, ci]
-    for m in range(3):
-        rows = slice(m * 128, (m + 1) * 128)
-        from_state_ref[rows, :] = (
+    for k in range(6):
+        lanes = slice(k * 256, (k + 1) * 256)
+        from_state_ref[:, lanes] = (
             jnp.dot(
-                previous_ref[rows, :].astype(bf16), state_ref[...], preferred_element_type=f32
-            )
-            + bias_ref[...]
+                previous_ref[...].astype(bf16), state_ref[:, lanes], preferred_element_type=f32
+            )
+            + state_bias_ref[:, lanes]
         )
-
-
-def state_part(hidden, state_gates, state_bias):
+    for source, target in ((gain_ref, gain_out), (shift_ref, shift_out)):
+        for half in range(2):
+            row = source[:, half * SIDE : (half + 1) * SIDE]
+            target[half * SIDE : (half + 1) * SIDE, :] = jnp.broadcast_to(row, (SIDE, SIDE)).T
+    for source, target in zip(vectors, vectors_out):
+        target[...] = source[...]
+    for copy in copies:
+        copy.wait()
+
+
+def ready(hidden, state_gates, state_bias, gain, shift, vectors, matrices):
     vmem = pl.BlockSpec(memory_space=pltpu.VMEM)
+    hbm = pl.BlockSpec(memory_space=pl.ANY)
+    shape = lambda v: jax.ShapeDtypeStruct(v.shape, v.dtype)
+    outs = [
+        jax.ShapeDtypeStruct((384, 512), f32),
+        jax.ShapeDtypeStruct((384, 1536), f32),
+        jax.ShapeDtypeStruct((256, SIDE), f32),
+        jax.ShapeDtypeStruct((256, SIDE), f32),
+        *map(shape, vectors),
+        *map(shape, matrices),
+    ]
     return pl.pallas_call(
-        state_kernel,
-        out_shape=(
-            jax.ShapeDtypeStruct((384, 512), f32),
-            jax.ShapeDtypeStruct((384, 1536), f32),
+        ready_kernel,
+        out_shape=outs,
+        in_specs=[vmem] * 10 + [hbm] * 4,
+        out_specs=[vmem] * len(outs),
+        scratch_shapes=[pltpu.SemaphoreType.DMA((4,))],
+        cost_estimate=pl.CostEstimate(
+            flops=2 * 384 * 512 * 1536, bytes_accessed=12000000, transcendentals=0
         ),
-        in_specs=[vmem] * 3,
-        out_specs=(vmem, vmem),
-        cost_estimate=pl.CostEstimate(
-            flops=2 * 384 * 512 * 1536, bytes_accessed=6000000, transcendentals=0
-        ),
-        compiler_params=pltpu.CompilerParams(vmem_limit_bytes=10 * 1024 * 1024),
-    )(hidden, state_gates, state_bias)
-
-
-def receive(message, *rest):
+        compiler_params=pltpu.CompilerParams(vmem_limit_bytes=14 * 1024 * 1024),
+    )(hidden, state_gates, state_bias, gain, shift, *vectors, *matrices)
+
+
+def receive(*operands):
     vmem = pl.BlockSpec(memory_space=pltpu.VMEM)
     return pl.pallas_call(
         receive_kernel,
@@ -359,7 +439,7 @@
             flops=2 * 700000000, bytes_accessed=8000000, transcendentals=2000000
         ),
         compiler_params=pltpu.CompilerParams(vmem_limit_bytes=20 * 1024 * 1024),
-    )(message, *rest)
+    )(*operands)
 
 
 def shards(
@@ -387,20 +467,29 @@
     message = message.reshape(128, 32, SIDE)
     arrived = lax.all_to_all(message, ("ty", "tx"), split_axis=0, concat_axis=0, tiled=True)
     row = lambda v: v.reshape(1, -1)
-    previous, from_state = state_part(hidden_state, state_gates, row(state_bias))
+    previous, from_state, gain, shift, *held = ready(
+        hidden_state,
+        state_gates,
+        row(state_bias),
+        row(norm_gain),
+        row(norm_shift),
+        [row(v) for v in (expand_bias, reduce_bias, layer_scale, project_bias, input_bias)],
+        [expand_weight, reduce_weight, project_weight, input_gates],
+    )
+    vectors, matrices = held[:5], held[5:]
     return receive(
         arrived.reshape(4096, SIDE),
-        row(norm_gain),
-        row(norm_shift),
-        expand_weight,
-        row(expand_bias),
-        reduce_weight,
-        row(reduce_bias),
-        row(layer_scale),
-        project_weight,
-        row(project_bias),
-        input_gates,
-        row(input_bias),
+        gain,
+        shift,
+        matrices[0],
+        vectors[0],
+        matrices[1],
+        vectors[1],
+        vectors[2],
+        matrices[2],
+        vectors[3],
+        matrices[3],
+        vectors[4],
         previous,
         from_state,
     )

time: 51.9 us -> 50.2 us (0.967)
  waiting for transfers between devices: 14.7 us -> 0.85 us
  local copies, waits for them, and re-layouts: 12.9 us -> 25.6 us
  Pallas kernels: 12.1 us -> 11.4 us
    all_to_all x1, waiting for transfers between devices: 14.7 us -> 0.85 us  [shards(): lax.all_to_all(message, ('ty', 'tx'), split_axis=0, concat_axis=0, tiled=...]
    unnamed x42 -> x64, local copies, waits for them, and re-layouts: 12.8 us -> 25.6 us
    pallas_call x2 -> x1, Pallas kernels: 2 us -> 1.03 us  [ready(): pl.pallas_call(ready_kernel, out_shape=outs, in_specs=[vmem] * 10 + [hbm]...]
    pallas_call x1, Pallas kernels: 4.71 us -> 5.42 us  [send(): pl.pallas_call(send_kernel, out_shape=jax.ShapeDtypeStruct((8, 16, 32, SI...]
where the time goes in v2:
time: 50.2 us; the launch traced here: 49.4 us
  local copies, waits for them, and re-layouts  25.6 us (51%)
  starting transfers between devices  11.5 us (23%)
  Pallas kernels  11.4 us (23%)
  waiting for transfers between devices  0.85 us (2%)
    unnamed x64, local copies, waits for them, and re-layouts  25.6 us
    all_to_all x1, starting transfers between devices, shards(): lax.all_to_all(message, ('ty', 'tx'), split_axis=0, concat_axis=0, tiled=...  11.5 us
    pallas_call x1, Pallas kernels, send(): pl.pallas_call(send_kernel, out_shape=jax.ShapeDtypeStruct((8, 16, 32, SI...  5.42 us
    pallas_call x1, Pallas kernels, receive(): pl.pallas_call(receive_kernel, out_shape=jax.ShapeDtypeStruct((FACES, 8,...  4.92 us
    pallas_call x1, Pallas kernels, ready(): pl.pallas_call(ready_kernel, out_shape=outs, in_specs=[vmem] * 10 + [hbm]...  1.03 us
  transfers between devices with their start and end apart: 1, of which 1 were waited for; matrix products, arithmetic and copies ran while one was open for 0% of the time, Pallas kernels for 2%

profile of v2, /device:TPU:1, one launch (start us, length us, event | category | flops | bytes accessed | tf_op | source)
XLA Modules:
  0.0 49.4 jit_solution(6874230374626385583)
XLA Ops:
  0.0 5.4 %shard_map.181 = bf16[8,16,32,128]{3,2,1,0:T(8,128)(2,1)} custom-call(f32[2,49]{1,0:T(2,128)} %bitcast.21, s32[4,12]{1,0:T(4,128)} %bitcast.19, s32[4,12]{1,0:T(4,128)} %bitcast.20, f32[2]{0:T(128)} %bias_hbm.1, bf16[2,12,128,128]{3,2,1,0:T(8,128)(2,1)} %x_hbm.1), custom_call_target="tpu_custom_call" | custom-call | flops 1610612736 | bytes 4000000 | tf_op jit(solution)/shard_map/pallas_call | solution.py:246
  5.5 11.5 %all-to-all-start = ((bf16[128,32,128]{2,1,0:T(8,128)(2,1)}), bf16[128,32,128]{2,1,0:T(8,128)(2,1)S(1)}, u32[]{:S(2)}, u32[]{:S(2)}) async-start(bf16[128,32,128]{2,1,0:T(8,128)(2,1)} %bitcast.18), calls=%async_computation | async-start | bytes 2097152 | tf_op jit(solution)/shard_map/all_to_all | solution.py:468
  17.0 1.4 %copy-done.2 = bf16[512,1536]{1,0:T(8,128)(2,1)S(1)} copy-done((bf16[512,1536]{1,0:T(8,128)(2,1)S(1)}, bf16[512,1536]{1,0:T(8,128)(2,1)}, u32[]{:S(2)}) %copy-start.2) | copy-done | bytes 1572888
  18.4 1.4 %copy-done.3 = bf16[512,1536]{1,0:T(8,128)(2,1)S(1)} copy-done((bf16[512,1536]{1,0:T(8,128)(2,1)S(1)}, bf16[512,1536]{1,0:T(8,128)(2,1)}, u32[]{:S(2)}) %copy-start.3) | copy-done | bytes 1572888
  19.9 1.1 %copy-done.6 = f32[12,8,4,512]{3,2,1,0:T(4,128)S(1)} copy-done((f32[12,8,4,512]{3,2,1,0:T(4,128)S(1)}, f32[12,8,4,512]{3,2,1,0:T(4,128)}, u32[]{:S(2)}) %copy-start.6) | copy-done | bytes 786456
  21.0 1.0 %copy-done.11 = bf16[256,1024]{1,0:T(8,128)(2,1)S(1)} copy-done((bf16[256,1024]{1,0:T(8,128)(2,1)S(1)}, bf16[256,1024]{1,0:T(8,128)(2,1)}, u32[]{:S(2)}) %copy-start.11) | copy-done | bytes 524312
  22.0 1.0 %copy-done.12 = bf16[1024,256]{1,0:T(8,128)(2,1)S(1)} copy-done((bf16[1024,256]{1,0:T(8,128)(2,1)S(1)}, bf16[1024,256]{1,0:T(8,128)(2,1)}, u32[]{:S(2)}) %copy-start.12) | copy-done | bytes 524312
  23.1 0.9 %copy-done.13 = bf16[256,512]{1,0:T(8,128)(2,1)S(1)} copy-done((bf16[256,512]{1,0:T(8,128)(2,1)S(1)}, bf16[256,512]{1,0:T(8,128)(2,1)}, u32[]{:S(2)}) %copy-start.13) | copy-done | bytes 262168
  24.0 0.7 %copy-done.19 = f32[512]{0:T(512)S(1)} copy-done((f32[512]{0:T(512)S(1)}, f32[512]{0:T(512)}, u32[]{:S(2)}) %copy-start.19) | copy-done | bytes 2072
  24.7 0.7 %copy-done.26 = f32[256]{0:T(256)S(1)} copy-done((f32[256]{0:T(256)S(1)}, f32[256]{0:T(256)}, u32[]{:S(2)}) %copy-start.26) | copy-done | bytes 1048
  27.4 1.0 %shard_map.182 = (f32[384,512]{1,0:T(8,128)S(1)}, f32[384,1536]{1,0:T(8,128)S(1)}, f32[256,128]{1,0:T(8,128)S(1)}, f32[256,128]{1,0:T(8,128)S(1)}, f32[1,1024]{1...) custom-call(f32[12,8,4,512]{3,2,1,0:T(4,128)S(1)} %copy-done.6, ...), custom_call_target="tpu_custom_call" | custom-call | flops 603979776 | bytes 12000000 | tf_op jit(solution)/shard_map/pallas_call | solution.py:412
  28.5 1.2 %copy-done = bf16[512,1536]{1,0:T(8,128)(2,1)} copy-done((bf16[512,1536]{1,0:T(8,128)(2,1)}, bf16[512,1536]{1,0:T(8,128)(2,1)S(1)}, u32[]{:S(2)}) %copy-start) | copy-done | bytes 1572888
  29.6 0.9 %copy-done.4 = f32[384,512]{1,0:T(8,128)} copy-done((f32[384,512]{1,0:T(8,128)}, f32[384,512]{1,0:T(8,128)S(1)}, u32[]{:S(2)}) %copy-start.4) | copy-done | bytes 786456
  30.5 0.8 %copy-done.7 = bf16[256,1024]{1,0:T(8,128)(2,1)} copy-done((bf16[256,1024]{1,0:T(8,128)(2,1)}, bf16[256,1024]{1,0:T(8,128)(2,1)S(1)}, u32[]{:S(2)}) %copy-start.7) | copy-done | bytes 524312
  31.3 0.8 %copy-done.9 = bf16[1024,256]{1,0:T(8,128)(2,1)} copy-done((bf16[1024,256]{1,0:T(8,128)(2,1)}, bf16[1024,256]{1,0:T(8,128)(2,1)S(1)}, u32[]{:S(2)}) %copy-start.9) | copy-done | bytes 524312
  32.1 0.7 %copy-done.14 = bf16[256,512]{1,0:T(8,128)(2,1)} copy-done((bf16[256,512]{1,0:T(8,128)(2,1)}, bf16[256,512]{1,0:T(8,128)(2,1)S(1)}, u32[]{:S(2)}) %copy-start.14) | copy-done | bytes 262168
  35.2 0.9 %all-to-all-done = bf16[128,32,128]{2,1,0:T(8,128)(2,1)S(1)} async-done(((bf16[128,32,128]{2,1,0:T(8,128)(2,1)}), bf16[128,32,128]{2,1,0:T(8,128)(2,1)S(1)}, u32[]{:S(2)}, u32[]{:S(2)}) %all-to-all-start) | async-done | bytes 1048608 | tf_op jit(solution)/shard_map/all_to_all | solution.py:468
  36.0 1.4 %copy-done.1 = bf16[512,1536]{1,0:T(8,128)(2,1)S(1)} copy-done((bf16[512,1536]{1,0:T(8,128)(2,1)S(1)}, bf16[512,1536]{1,0:T(8,128)(2,1)}, u32[]{:S(2)}) %copy-start.1) | copy-done | bytes 1572888
  37.5 1.1 %copy-done.5 = f32[384,512]{1,0:T(8,128)S(1)} copy-done((f32[384,512]{1,0:T(8,128)S(1)}, f32[384,512]{1,0:T(8,128)}, u32[]{:S(2)}) %copy-start.5) | copy-done | bytes 786456
  38.6 1.0 %copy-done.8 = bf16[256,1024]{1,0:T(8,128)(2,1)S(1)} copy-done((bf16[256,1024]{1,0:T(8,128)(2,1)S(1)}, bf16[256,1024]{1,0:T(8,128)(2,1)}, u32[]{:S(2)}) %copy-start.8) | copy-done | bytes 524312
  39.6 1.0 %copy-done.10 = bf16[1024,256]{1,0:T(8,128)(2,1)S(1)} copy-done((bf16[1024,256]{1,0:T(8,128)(2,1)S(1)}, bf16[1024,256]{1,0:T(8,128)(2,1)}, u32[]{:S(2)}) %copy-start.10) | copy-done | bytes 524312
  40.7 0.9 %copy-done.15 = bf16[256,512]{1,0:T(8,128)(2,1)S(1)} copy-done((bf16[256,512]{1,0:T(8,128)(2,1)S(1)}, bf16[256,512]{1,0:T(8,128)(2,1)}, u32[]{:S(2)}) %copy-start.15) | copy-done | bytes 262168
  41.6 0.9 %copy-done.17 = f32[256,128]{1,0:T(8,128)S(1)} copy-done((f32[256,128]{1,0:T(8,128)S(1)}, f32[256,128]{1,0:T(8,128)}, u32[]{:S(2)}) %copy-start.17) | copy-done | bytes 131096
  44.5 4.9 %shard_map.183 = f32[12,8,4,512]{3,2,1,0:T(4,128)} custom-call(bf16[4096,128]{1,0:T(8,128)(2,1)S(1)} %bitcast.11, f32[256,128]{1,0:T(8,128)S(1)} %get-tuple-element.18.gain_ref, f32[256,128]{1,0:T(8,128)S(1)} %copy-done.17, bf16[256,1024]{1,0:T(8,128)(2,1)S(1)} %copy-done.8, f32[1,1024]{1,0:T(1,128)S(1)} %get-tuple-element.21.expand_bias_ref, ...), custom_call_target="tpu_custom_call" | custom-call | flops 1400000000 | bytes 8000000 | tf_op jit(solution)/shard_map/pallas_call | solution.py:427
  (47 shorter events, 6.5 us)
Async XLA Ops:
  5.4 11.6 %copy-start.30 = (f32[1536]{0:T(1024)S(1)}, f32[1536]{0:T(1024)}, u32[]{:S(2)}) copy-start(f32[1536]{0:T(1024)} %param.34) | copy-start | bytes 18436
  5.4 11.6 %copy-start.31 = (f32[1536]{0:T(1024)S(1)}, f32[1536]{0:T(1024)}, u32[]{:S(2)}) copy-start(f32[1536]{0:T(1024)} %param.36) | copy-start | bytes 18436
  5.4 11.6 %copy-start.18 = (f32[1024]{0:T(1024)S(1)}, f32[1024]{0:T(1024)}, u32[]{:S(2)}) copy-start(f32[1024]{0:T(1024)} %param.27) | copy-start | bytes 12292
  5.5 30.6 %all-to-all-start = ((bf16[128,32,128]{2,1,0:T(8,128)(2,1)}), bf16[128,32,128]{2,1,0:T(8,128)(2,1)S(1)}, u32[]{:S(2)}, u32[]{:S(2)}) async-start(bf16[128,32,128]{2,1,0:T(8,128)(2,1)} %bitcast.18), calls=%async_computation | async-start | bytes 2097152 | tf_op jit(solution)/shard_map/all_to_all | solution.py:468
  17.0 1.4 %copy-start.2 = (bf16[512,1536]{1,0:T(8,128)(2,1)S(1)}, bf16[512,1536]{1,0:T(8,128)(2,1)}, u32[]{:S(2)}) copy-start(bf16[512,1536]{1,0:T(8,128)(2,1)} %refs_1_.1) | copy-start | bytes 4718596
  18.4 1.4 %copy-start.3 = (bf16[512,1536]{1,0:T(8,128)(2,1)S(1)}, bf16[512,1536]{1,0:T(8,128)(2,1)}, u32[]{:S(2)}) copy-start(bf16[512,1536]{1,0:T(8,128)(2,1)} %refs_13_.1) | copy-start | bytes 4718596
  19.9 1.1 %copy-start.6 = (f32[12,8,4,512]{3,2,1,0:T(4,128)S(1)}, f32[12,8,4,512]{3,2,1,0:T(4,128)}, u32[]{:S(2)}) copy-start(f32[12,8,4,512]{3,2,1,0:T(4,128)} %refs_0_.1) | copy-start | bytes 2359300
  21.0 1.0 %copy-start.11 = (bf16[256,1024]{1,0:T(8,128)(2,1)S(1)}, bf16[256,1024]{1,0:T(8,128)(2,1)}, u32[]{:S(2)}) copy-start(bf16[256,1024]{1,0:T(8,128)(2,1)} %refs_10_.1) | copy-start | bytes 1572868
  22.0 1.0 %copy-start.12 = (bf16[1024,256]{1,0:T(8,128)(2,1)S(1)}, bf16[1024,256]{1,0:T(8,128)(2,1)}, u32[]{:S(2)}) copy-start(bf16[1024,256]{1,0:T(8,128)(2,1)} %refs_11_.1) | copy-start | bytes 1572868
  23.1 0.9 %copy-start.13 = (bf16[256,512]{1,0:T(8,128)(2,1)S(1)}, bf16[256,512]{1,0:T(8,128)(2,1)}, u32[]{:S(2)}) copy-start(bf16[256,512]{1,0:T(8,128)(2,1)} %refs_12_.1) | copy-start | bytes 786436
  24.0 0.7 %copy-start.19 = (f32[512]{0:T(512)S(1)}, f32[512]{0:T(512)}, u32[]{:S(2)}) copy-start(f32[512]{0:T(512)} %param.32) | copy-start | bytes 6148
  24.7 0.7 %copy-start.26 = (f32[256]{0:T(256)S(1)}, f32[256]{0:T(256)}, u32[]{:S(2)}) copy-start(f32[256]{0:T(256)} %param.24) | copy-start | bytes 3076
  25.4 0.7 %copy-start.27 = (f32[256]{0:T(256)S(1)}, f32[256]{0:T(256)}, u32[]{:S(2)}) copy-start(f32[256]{0:T(256)} %param.25) | copy-start | bytes 3076
  28.5 1.2 %copy-start = (bf16[512,1536]{1,0:T(8,128)(2,1)}, bf16[512,1536]{1,0:T(8,128)(2,1)S(1)}, u32[]{:S(2)}) copy-start(bf16[512,1536]{1,0:T(8,128)(2,1)S(1)} %get-tuple-element.27.input_ref) | copy-start | bytes 4718596
  29.6 0.9 %copy-start.4 = (f32[384,512]{1,0:T(8,128)}, f32[384,512]{1,0:T(8,128)S(1)}, u32[]{:S(2)}) copy-start(f32[384,512]{1,0:T(8,128)S(1)} %get-tuple-element.29.previous_ref) | copy-start | bytes 2359300
  30.5 0.8 %copy-start.7 = (bf16[256,1024]{1,0:T(8,128)(2,1)}, bf16[256,1024]{1,0:T(8,128)(2,1)S(1)}, u32[]{:S(2)}) copy-start(bf16[256,1024]{1,0:T(8,128)(2,1)S(1)} %get-tuple-element.20.expand_ref) | copy-start | bytes 1572868
  31.3 0.8 %copy-start.9 = (bf16[1024,256]{1,0:T(8,128)(2,1)}, bf16[1024,256]{1,0:T(8,128)(2,1)S(1)}, u32[]{:S(2)}) copy-start(bf16[1024,256]{1,0:T(8,128)(2,1)S(1)} %get-tuple-element.22.reduce_ref) | copy-start | bytes 1572868
  32.1 0.7 %copy-start.14 = (bf16[256,512]{1,0:T(8,128)(2,1)}, bf16[256,512]{1,0:T(8,128)(2,1)S(1)}, u32[]{:S(2)}) copy-start(bf16[256,512]{1,0:T(8,128)(2,1)S(1)} %get-tuple-element.25.project_ref) | copy-start | bytes 786436
  36.0 1.4 %copy-start.1 = (bf16[512,1536]{1,0:T(8,128)(2,1)S(1)}, bf16[512,1536]{1,0:T(8,128)(2,1)}, u32[]{:S(2)}) copy-start(bf16[512,1536]{1,0:T(8,128)(2,1)} %copy-done) | copy-start | bytes 4718596
  37.4 1.1 %copy-start.5 = (f32[384,512]{1,0:T(8,128)S(1)}, f32[384,512]{1,0:T(8,128)}, u32[]{:S(2)}) copy-start(f32[384,512]{1,0:T(8,128)} %copy-done.4) | copy-start | bytes 2359300
  38.6 1.0 %copy-start.8 = (bf16[256,1024]{1,0:T(8,128)(2,1)S(1)}, bf16[256,1024]{1,0:T(8,128)(2,1)}, u32[]{:S(2)}) copy-start(bf16[256,1024]{1,0:T(8,128)(2,1)} %copy-done.7) | copy-start | bytes 1572868
  39.6 1.0 %copy-start.10 = (bf16[1024,256]{1,0:T(8,128)(2,1)S(1)}, bf16[1024,256]{1,0:T(8,128)(2,1)}, u32[]{:S(2)}) copy-start(bf16[1024,256]{1,0:T(8,128)(2,1)} %copy-done.9) | copy-start | bytes 1572868
  40.7 0.9 %copy-start.15 = (bf16[256,512]{1,0:T(8,128)(2,1)S(1)}, bf16[256,512]{1,0:T(8,128)(2,1)}, u32[]{:S(2)}) copy-start(bf16[256,512]{1,0:T(8,128)(2,1)} %copy-done.14) | copy-start | bytes 786436
  41.6 0.9 %copy-start.17 = (f32[256,128]{1,0:T(8,128)S(1)}, f32[256,128]{1,0:T(8,128)}, u32[]{:S(2)}) copy-start(f32[256,128]{1,0:T(8,128)} %copy-done.16) | copy-start | bytes 393220
  (9 other events, 5.7 us)

commit v3 on v2

--- a/solution.py
+++ b/solution.py
@@ -12,7 +12,10 @@
 PADDED = SIDE + 16
 DEPTH = (KERNEL + 1) * SIDE
 
-SEND_VMEM = 63 * 1024 * 1024
+VMEM_LIMIT = 63 * 1024 * 1024
+RECEIVE_VMEM = 44 * 1024 * 1024
+WEIGHT_ROWS = 8192
+STATE_FACES = 34 * FACES
 
 f32 = jnp.float32
 bf16 = jnp.bfloat16
@@ -269,35 +272,56 @@
         cost_estimate=pl.CostEstimate(
             flops=2 * 2 * 1536 * DEPTH * 256, bytes_accessed=4000000, transcendentals=0
         ),
-        compiler_params=pltpu.CompilerParams(vmem_limit_bytes=SEND_VMEM),
+        compiler_params=pltpu.CompilerParams(vmem_limit_bytes=VMEM_LIMIT),
     )(conv_kernel.T, neighbour_face.T, neighbour_side.T, conv_bias, features)
 
 
 def receive_kernel(
     msg_ref,
-    gain_ref,
-    shift_ref,
+    vector_ref,
+    from_state_ref,
+    weight_hbm,
+    held_hbm,
+    out_hbm,
     expand_ref,
-    expand_bias_ref,
     reduce_ref,
-    reduce_bias_ref,
-    scale_ref,
     project_ref,
-    project_bias_ref,
     input_ref,
-    input_bias_ref,
-    previous_ref,
-    from_state_ref,
+    hidden_ref,
     out_ref,
     wide_ref,
     normed_ref,
     pooled_ref,
     units_ref,
+    sems,
+    out_sem,
 ):
+    operands = [
+        (expand_part(weight_hbm), expand_ref),
+        (reduce_part(weight_hbm), reduce_ref),
+        (project_part(weight_hbm), project_ref),
+        (input_part(weight_hbm), input_ref),
+        (held_hbm.at[pl.ds(0, FACES)], hidden_ref),
+    ]
+    loads = [
+        pltpu.make_async_copy(source, target, sems.at[k])
+        for k, (source, target) in enumerate(operands)
+    ]
+    for copy in loads:
+        copy.start()
+
+    def vector(k, lanes):
+        return vector_ref[k : k + 1, lanes]
+
+    def column(k):
+        row = vector(k, slice(0, 256))
+        halves = [row[:, :SIDE], row[:, SIDE:]]
+        return jnp.concatenate([jnp.broadcast_to(v, (SIDE, SIDE)).T for v in halves], axis=0)
+
+    gain = column(5)
+    shift = column(6)
     wide_ref[...] = msg_ref[...].astype(f32)
     lane = iota((256, SIDE), 1)
-    gain = gain_ref[...]
-    shift = shift_ref[...]
     for r in range(16):
         di, ci = r // 8, r % 8
         values = wide_ref[pl.ds(r, 256, stride=16), :]
@@ -311,6 +335,7 @@
         normed_ref[di * 2 + 1, rows, :] = cells[48:96]
         pooled_ref[ci * 48 + di * 24 : ci * 48 + (di + 1) * 24, :] = cells[96:].astype(f32)[:24]
 
+    loads[0].wait()
     for k in range(4):
         lanes = slice(k * 256, (k + 1) * 256)
         for m in range(3):
@@ -322,19 +347,24 @@
             )
             total = None
             for s in range(4):
-                part = hidden[s * 128 : (s + 1) * 128] + expand_bias_ref[:, lanes]
+                part = hidden[s * 128 : (s + 1) * 128] + vector(0, lanes)
                 unit = part * (1.0 + lax.erf(part * (0.5**0.5)))
                 total = unit if total is None else total + unit
             units_ref[rows, lanes] = total.astype(bf16)
 
+    loads[1].wait()
+    loads[2].wait()
     update = (
         jnp.dot(units_ref[...], reduce_ref[...], preferred_element_type=f32) * 0.125
-        + reduce_bias_ref[...]
-    ) * scale_ref[...]
+        + vector(1, slice(0, 256))
+    ) * vector(2, slice(0, 256))
     pooled = (pooled_ref[...] + update).astype(bf16)
     mapped = (
-        jnp.dot(pooled, project_ref[...], preferred_element_type=f32) + project_bias_ref[...]
+        jnp.dot(pooled, project_ref[...], preferred_element_type=f32) + vector(3, slice(0, 512))
     ).astype(bf16)
+
+    for copy in loads[3:]:
+        copy.wait()
 
     def sigmoid(v):
         return 0.5 * jnp.tanh(0.5 * v) + 0.5
@@ -345,7 +375,7 @@
             lanes = slice(block * 512 + k * 256, block * 512 + (k + 1) * 256)
             return (
                 jnp.dot(mapped, input_ref[:, lanes], preferred_element_type=f32)
-                + input_bias_ref[:, lanes],
+                + vector(4, lanes),
                 from_state_ref[:, lanes],
             )
 
@@ -356,25 +386,101 @@
         reset_gate = sigmoid(a + b)
         a, b = gate(2)
         candidate = jnp.tanh(a + reset_gate * b)
-        new = candidate + update_gate * (previous_ref[:, lanes] - candidate)
         for ci in range(8):
             for f in range(FACES):
-                at = ci * 48 + f * 4
-                out_ref[f, ci, :, lanes] = new[at : at + 4]
-
-
-def ready_kernel(*refs):
-    hidden_ref, state_ref, state_bias_ref, gain_ref, shift_ref = refs[:5]
-    vectors, matrices = refs[5:10], refs[10:14]
-    previous_ref, from_state_ref, gain_out, shift_out = refs[14:18]
-    vectors_out, matrices_out = refs[18:23], refs[23:27]
-    sems = refs[27]
-    copies = [
+                rows = slice(ci * 48 + f * 4, ci * 48 + f * 4 + 4)
+                kept = candidate[rows]
+                out_ref[f, ci, :, lanes] = kept + update_gate[rows] * (
+                    hidden_ref[f, ci, :, lanes] - kept
+                )
+    copy = pltpu.make_async_copy(out_ref, out_hbm, out_sem)
+    copy.start()
+    copy.wait()
+
+
+def input_part(ref):
+    return ref.at[pl.ds(0, 512)]
+
+
+def expand_part(ref):
+    return ref.at[pl.ds(512, 256), pl.ds(0, 1024)]
+
+
+def project_part(ref):
+    return ref.at[pl.ds(512, 256), pl.ds(1024, 512)]
+
+
+def reduce_part(ref):
+    return ref.at[pl.ds(768, 1024), pl.ds(0, 256)]
+
+
+def ready_kernel(
+    hidden_hbm,
+    state_hbm,
+    state_bias_hbm,
+    gain_hbm,
+    shift_hbm,
+    expand_bias_hbm,
+    reduce_bias_hbm,
+    scale_hbm,
+    project_bias_hbm,
+    input_bias_hbm,
+    expand_hbm,
+    reduce_hbm,
+    project_hbm,
+    input_hbm,
+    from_state_ref,
+    vector_ref,
+    weight_hbm,
+    held_hbm,
+    hidden_ref,
+    state_ref,
+    state_bias_ref,
+    gain_ref,
+    shift_ref,
+    expand_bias_ref,
+    reduce_bias_ref,
+    scale_ref,
+    project_bias_ref,
+    input_bias_ref,
+    previous_ref,
+    sems,
+    pack_sems,
+):
+    packs = [
+        pltpu.make_async_copy(source, target, pack_sems.at[k])
+        for k, (source, target) in enumerate(
+            [
+                (expand_hbm, expand_part(weight_hbm)),
+                (reduce_hbm, reduce_part(weight_hbm)),
+                (project_hbm, project_part(weight_hbm)),
+                (input_hbm, input_part(weight_hbm)),
+                (hidden_hbm, held_hbm.at[pl.ds(0, FACES)]),
+            ]
+        )
+    ]
+    for copy in packs:
+        copy.start()
+    operands = [
+        (hidden_hbm, hidden_ref),
+        (state_hbm, state_ref),
+        (state_bias_hbm, state_bias_ref),
+        (gain_hbm, gain_ref),
+        (shift_hbm, shift_ref),
+        (expand_bias_hbm, expand_bias_ref),
+        (reduce_bias_hbm, reduce_bias_ref),
+        (scale_hbm, scale_ref),
+        (project_bias_hbm, project_bias_ref),
+        (input_bias_hbm, input_bias_ref),
+    ]
+    loads = [
         pltpu.make_async_copy(source, target, sems.at[k])
-        for k, (source, target) in enumerate(zip(matrices, matrices_out))
+        for k, (source, target) in enumerate(operands)
     ]
-    for copy in copies:
+    for copy in loads:
         copy.start()
+    for copy in loads:
+        copy.wait()
     for ci in range(8):
         for f in range(FACES):
             at = ci * 48 + f * 4
@@ -387,59 +493,76 @@
             )
             + state_bias_ref[:, lanes]
         )
-    for source, target in ((gain_ref, gain_out), (shift_ref, shift_out)):
-        for half in range(2):
-            row = source[:, half * SIDE : (half + 1) * SIDE]
-            target[half * SIDE : (half + 1) * SIDE, :] = jnp.broadcast_to(row, (SIDE, SIDE)).T
-    for source, target in zip(vectors, vectors_out):
-        target[...] = source[...]
-    for copy in copies:
+    vectors = (
+        expand_bias_ref,
+        reduce_bias_ref,
+        scale_ref,
+        project_bias_ref,
+        input_bias_ref,
+        gain_ref,
+        shift_ref,
+    )
+    for k, source in enumerate(vectors):
+        vector_ref[k : k + 1, : source.shape[1]] = source[...]
+    for copy in packs:
         copy.wait()
 
 
-def ready(hidden, state_gates, state_bias, gain, shift, vectors, matrices):
+def ready(hidden, state_gates, vectors, weights):
     vmem = pl.BlockSpec(memory_space=pltpu.VMEM)
     hbm = pl.BlockSpec(memory_space=pl.ANY)
-    shape = lambda v: jax.ShapeDtypeStruct(v.shape, v.dtype)
-    outs = [
-        jax.ShapeDtypeStruct((384, 512), f32),
-        jax.ShapeDtypeStruct((384, 1536), f32),
-        jax.ShapeDtypeStruct((256, SIDE), f32),
-        jax.ShapeDtypeStruct((256, SIDE), f32),
-        *map(shape, vectors),
-        *map(shape, matrices),
-    ]
+    operands = (hidden, state_gates) + tuple(v.reshape(1, -1) for v in vectors)
     return pl.pallas_call(
         ready_kernel,
-        out_shape=outs,
-        in_specs=[vmem] * 10 + [hbm] * 4,
-        out_specs=[vmem] * len(outs),
-        scratch_shapes=[pltpu.SemaphoreType.DMA((4,))],
+        out_shape=(
+            jax.ShapeDtypeStruct((384, 1536), f32),
+            jax.ShapeDtypeStruct((8, 1536), f32),
+            jax.ShapeDtypeStruct((WEIGHT_ROWS, 1536), bf16),
+            jax.ShapeDtypeStruct((STATE_FACES, 8, 4, 512), f32),
+        ),
+        in_specs=[hbm] * (len(operands) + len(weights)),
+        out_specs=(vmem, vmem, hbm, hbm),
+        scratch_shapes=[pltpu.VMEM(v.shape, v.dtype) for v in operands]
+        + [
+            pltpu.VMEM((384, 512), f32),
+            pltpu.SemaphoreType.DMA((len(operands),)),
+            pltpu.SemaphoreType.DMA((5,)),
+        ],
         cost_estimate=pl.CostEstimate(
-            flops=2 * 384 * 512 * 1536, bytes_accessed=12000000, transcendentals=0
+            flops=2 * 384 * 512 * 1536, bytes_accessed=8000000, transcendentals=0
         ),
-        compiler_params=pltpu.CompilerParams(vmem_limit_bytes=14 * 1024 * 1024),
-    )(hidden, state_gates, state_bias, gain, shift, *vectors, *matrices)
-
-
-def receive(*operands):
+        compiler_params=pltpu.CompilerParams(vmem_limit_bytes=RECEIVE_VMEM),
+    )(*operands, *weights)
+
+
+def receive(message, vectors, from_state, weights, held):
     vmem = pl.BlockSpec(memory_space=pltpu.VMEM)
+    hbm = pl.BlockSpec(memory_space=pl.ANY)
+    result = jax.ShapeDtypeStruct((FACES, 8, 4, 512), f32)
     return pl.pallas_call(
         receive_kernel,
-        out_shape=jax.ShapeDtypeStruct((FACES, 8, 4, 512), f32),
-        in_specs=[vmem] * 14,
-        out_specs=vmem,
+        out_shape=result,
+        in_specs=[vmem, vmem, vmem, hbm, hbm],
+        out_specs=hbm,
         scratch_shapes=[
+            pltpu.VMEM((256, 1024), bf16),
+            pltpu.VMEM((1024, 256), bf16),
+            pltpu.VMEM((256, 512), bf16),
+            pltpu.VMEM((512, 1536), bf16),
+            pltpu.VMEM(result.shape, f32),
+            pltpu.VMEM(result.shape, f32),
             pltpu.VMEM((4096, SIDE), f32),
             pltpu.VMEM((4, 384, 256), bf16),
             pltpu.VMEM((384, 256), f32),
             pltpu.VMEM((384, 1024), bf16),
+            pltpu.SemaphoreType.DMA((5,)),
+            pltpu.SemaphoreType.DMA,
         ],
         cost_estimate=pl.CostEstimate(
             flops=2 * 700000000, bytes_accessed=8000000, transcendentals=2000000
         ),
-        compiler_params=pltpu.CompilerParams(vmem_limit_bytes=20 * 1024 * 1024),
-    )(*operands)
+        compiler_params=pltpu.CompilerParams(vmem_limit_bytes=RECEIVE_VMEM),
+    )(message, vectors, from_state, weights, held)
 
 
 def shards(
@@ -466,33 +589,22 @@
     message = send(features, conv_kernel, conv_bias, neighbour_face, neighbour_side)
     message = message.reshape(128, 32, SIDE)
     arrived = lax.all_to_all(message, ("ty", "tx"), split_axis=0, concat_axis=0, tiled=True)
-    row = lambda v: v.reshape(1, -1)
-    previous, from_state, gain, shift, *held = ready(
+    from_state, vectors, weights, held = ready(
         hidden_state,
         state_gates,
-        row(state_bias),
-        row(norm_gain),
-        row(norm_shift),
-        [row(v) for v in (expand_bias, reduce_bias, layer_scale, project_bias, input_bias)],
-        [expand_weight, reduce_weight, project_weight, input_gates],
+        (
+            state_bias,
+            norm_gain,
+            norm_shift,
+            expand_bias,
+            reduce_bias,
+            layer_scale,
+            project_bias,
+            input_bias,
+        ),
+        (expand_weight, reduce_weight, project_weight, input_gates),
     )
-    vectors, matrices = held[:5], held[5:]
-    return receive(
-        arrived.reshape(4096, SIDE),
-        gain,
-        shift,
-        matrices[0],
-        vectors[0],
-        matrices[1],
-        vectors[1],
-        vectors[2],
-        matrices[2],
-        vectors[3],
-        matrices[3],
-        vectors[4],
-        previous,
-        from_state,
-    )
+    return receive(arrived.reshape(4096, SIDE), vectors, from_state, weights, held)
 
 
 def solution(mesh):

time: 50.2 us -> 42.3 us (0.84)
  local copies, waits for them, and re-layouts: 25.6 us -> 7.02 us
  waiting for transfers between devices: 0.85 us -> 10 us
  Pallas kernels: 11.4 us -> 13.2 us
    unnamed x64 -> x28, local copies, waits for them, and re-layouts: 25.6 us -> 7.01 us
    all_to_all x1, waiting for transfers between devices: 0.85 us -> 10 us  [shards(): lax.all_to_all(message, ('ty', 'tx'), split_axis=0, concat_axis=0, tiled=...]
    pallas_call x2, Pallas kernels: 5.95 us -> 7.71 us  [the longest x1 5.76 us: receive(): pl.pallas_call(receive_kernel, out_shape=result, in_specs=[vmem, vmem, vm...]
  transfers between devices with their start and end apart: 1 -> 1, of which waited for: 1 -> 1; matrix products, arithmetic and copies ran while one was open for 0% -> 0% of each run, Pallas kernels for 2% -> 5%
where the time goes in v3:
time: 42.3 us; the launch traced here: 41.8 us
  Pallas kernels  13.2 us (31%)
  starting transfers between devices  11.5 us (27%)
  waiting for transfers between devices  10 us (24%)
  local copies, waits for them, and re-layouts  7.02 us (17%)
    all_to_all x1, starting transfers between devices, shards(): lax.all_to_all(message, ('ty', 'tx'), split_axis=0, concat_axis=0, tiled=...  11.5 us
    all_to_all x1, waiting for transfers between devices, shards(): lax.all_to_all(message, ('ty', 'tx'), split_axis=0, concat_axis=0, tiled=...  10 us
    unnamed x28, local copies, waits for them, and re-layouts  7.01 us
    pallas_call x1, Pallas kernels, receive(): pl.pallas_call(receive_kernel, out_shape=result, in_specs=[vmem, vmem, vm...  5.76 us
    pallas_call x1, Pallas kernels, send(): pl.pallas_call(send_kernel, out_shape=jax.ShapeDtypeStruct((8, 16, 32, SI...  5.45 us
    pallas_call x1, Pallas kernels, ready(): pl.pallas_call(ready_kernel, out_shape=(jax.ShapeDtypeStruct((384, 1536),...  1.96 us
  transfers between devices with their start and end apart: 1, of which 1 were waited for; matrix products, arithmetic and copies ran while one was open for 0% of the time, Pallas kernels for 5%

profile of v3, /device:TPU:1, one launch (start us, length us, event | category | flops | bytes accessed | tf_op | source)
XLA Modules:
  0.0 41.8 jit_solution(8061566693423629262)
XLA Ops:
  0.0 0.0 copy-start.7
  0.0 0.0 copy-start.8
  0.0 0.0 copy-start.9
  0.0 0.0 copy-start.10
  0.0 0.0 copy-start.11
  0.1 5.4 %shard_map.181 = bf16[8,16,32,128]{3,2,1,0:T(8,128)(2,1)} custom-call(f32[2,49]{1,0:T(2,128)} %bitcast.21, s32[4,12]{1,0:T(4,128)} %bitcast.19, s32[4,12]{1,0:T(4,128)} %bitcast.20, f32[2]{0:T(128)} %bias_hbm.1, bf16[2,12,128,128]{3,2,1,0:T(8,128)(2,1)} %x_hbm.1), custom_call_target="tpu_custom_call" | custom-call | flops 1610612736 | bytes 4000000 | tf_op jit(solution)/shard_map/pallas_call | solution.py:249
  5.5 11.5 %all-to-all-start = ((bf16[128,32,128]{2,1,0:T(8,128)(2,1)}), bf16[128,32,128]{2,1,0:T(8,128)(2,1)S(1)}, u32[]{:S(2)}, u32[]{:S(2)}) async-start(bf16[128,32,128]{2,1,0:T(8,128)(2,1)} %bitcast.18), calls=%async_computation | async-start | bytes 2097152 | tf_op jit(solution)/shard_map/all_to_all | solution.py:591
  17.0 0.0 copy-done.12
  17.0 0.0 copy-done.13
  17.1 0.0 copy-done.6
  17.1 0.0 copy-done.7
  17.1 0.0 copy-done.8
  17.1 0.0 copy-done.9
  17.1 0.0 copy-done.10
  17.1 0.0 copy-start
  17.1 1.4 %copy-done = bf16[512,1536]{1,0:T(8,128)(2,1)S(1)} copy-done((bf16[512,1536]{1,0:T(8,128)(2,1)S(1)}, bf16[512,1536]{1,0:T(8,128)(2,1)}, u32[]{:S(2)}) %copy-start) | copy-done | bytes 1572888
  18.5 1.4 %copy-done.1 = bf16[512,1536]{1,0:T(8,128)(2,1)S(1)} copy-done((bf16[512,1536]{1,0:T(8,128)(2,1)S(1)}, bf16[512,1536]{1,0:T(8,128)(2,1)}, u32[]{:S(2)}) %copy-start.1) | copy-done | bytes 1572888
  20.0 1.1 %copy-done.2 = f32[12,8,4,512]{3,2,1,0:T(4,128)S(1)} copy-done((f32[12,8,4,512]{3,2,1,0:T(4,128)S(1)}, f32[12,8,4,512]{3,2,1,0:T(4,128)}, u32[]{:S(2)}) %copy-start.2) | copy-done | bytes 786456
  21.1 1.0 %copy-done.3 = bf16[256,1024]{1,0:T(8,128)(2,1)S(1)} copy-done((bf16[256,1024]{1,0:T(8,128)(2,1)S(1)}, bf16[256,1024]{1,0:T(8,128)(2,1)}, u32[]{:S(2)}) %copy-start.3) | copy-done | bytes 524312
  22.1 1.0 %copy-done.4 = bf16[1024,256]{1,0:T(8,128)(2,1)S(1)} copy-done((bf16[1024,256]{1,0:T(8,128)(2,1)S(1)}, bf16[1024,256]{1,0:T(8,128)(2,1)}, u32[]{:S(2)}) %copy-start.4) | copy-done | bytes 524312
  23.2 0.9 %copy-done.5 = bf16[256,512]{1,0:T(8,128)(2,1)S(1)} copy-done((bf16[256,512]{1,0:T(8,128)(2,1)S(1)}, bf16[256,512]{1,0:T(8,128)(2,1)}, u32[]{:S(2)}) %copy-start.5) | copy-done | bytes 262168
  24.1 2.0 %shard_map.182 = (f32[384,1536]{1,0:T(8,128)S(1)}, f32[8,1536]{1,0:T(8,128)S(1)}, bf16[8192,1536]{1,0:T(8,128)(2,1)}, f32[408,8,4,512]{3,2,1,0:T(4,128)}) custom-call(f32[12,8,4,512]{3,2,1,0:T(4,128)S(1)} %copy-done.2, bf16[512,1536]{1,0:T(8,128)(2,1)S(1)} %copy-done, f32[1,1536]{1,0:T(1,128)S(1)} %reshape.32.state_bias_hbm, f32[1,256]{1,0:T(1,128)S(1)} %bitcast.14, ...), custom_call_target="tpu_custom_call" | custom-call | flops 603979776 | bytes 8000000 | tf_op jit(solution)/shard_map/pallas_call | solution.py:515
  26.1 10.0 %all-to-all-done = bf16[128,32,128]{2,1,0:T(8,128)(2,1)S(1)} async-done(((bf16[128,32,128]{2,1,0:T(8,128)(2,1)}), bf16[128,32,128]{2,1,0:T(8,128)(2,1)S(1)}, u32[]{:S(2)}, u32[]{:S(2)}) %all-to-all-start) | async-done | bytes 1048608 | tf_op jit(solution)/shard_map/all_to_all | solution.py:591
  36.1 5.8 %shard_map.183 = f32[12,8,4,512]{3,2,1,0:T(4,128)} custom-call(bf16[4096,128]{1,0:T(8,128)(2,1)S(1)} %bitcast.11, f32[8,1536]{1,0:T(8,128)S(1)} %get-tuple-element.9.vector_ref, f32[384,1536]{1,0:T(8,128)S(1)} %get-tuple-element.10.from_state_ref, bf16[8192,1536]{1,0:T(8,128)(2,1)} %get-tuple-element.11.weight_hbm, f32[408,8,4,512]{3,2,1,0:T(4,128)} %get-tuple-element.12.held_hbm), custom_call_target="tpu_custom_call" | custom-call | flops 1400000000 | bytes 8000000 | tf_op jit(solution)/shard_map/pallas_call | solution.py:542
  (11 shorter events, 0.0 us)
Async XLA Ops:
  0.0 17.0 %copy-start.12 = (f32[1536]{0:T(1024)S(1)}, f32[1536]{0:T(1024)}, u32[]{:S(2)}) copy-start(f32[1536]{0:T(1024)} %param.34) | copy-start | bytes 18436
  0.0 17.0 %copy-start.13 = (f32[1536]{0:T(1024)S(1)}, f32[1536]{0:T(1024)}, u32[]{:S(2)}) copy-start(f32[1536]{0:T(1024)} %param.36) | copy-start | bytes 18436
  0.0 17.1 %copy-start.6 = (f32[1024]{0:T(1024)S(1)}, f32[1024]{0:T(1024)}, u32[]{:S(2)}) copy-start(f32[1024]{0:T(1024)} %param.27) | copy-start | bytes 12292
  0.0 17.1 %copy-start.7 = (f32[512]{0:T(512)S(1)}, f32[512]{0:T(512)}, u32[]{:S(2)}) copy-start(f32[512]{0:T(512)} %param.32) | copy-start | bytes 6148
  0.0 17.1 %copy-start.8 = (f32[256]{0:T(256)S(1)}, f32[256]{0:T(256)}, u32[]{:S(2)}) copy-start(f32[256]{0:T(256)} %param.24) | copy-start | bytes 3076
  0.0 17.1 %copy-start.9 = (f32[256]{0:T(256)S(1)}, f32[256]{0:T(256)}, u32[]{:S(2)}) copy-start(f32[256]{0:T(256)} %param.25) | copy-start | bytes 3076
  0.0 17.1 %copy-start.10 = (f32[256]{0:T(256)S(1)}, f32[256]{0:T(256)}, u32[]{:S(2)}) copy-start(f32[256]{0:T(256)} %param.29) | copy-start | bytes 3076
  0.0 17.1 %copy-start.11 = (f32[256]{0:T(256)S(1)}, f32[256]{0:T(256)}, u32[]{:S(2)}) copy-start(f32[256]{0:T(256)} %param.30) | copy-start | bytes 3076
  5.5 30.6 %all-to-all-start = ((bf16[128,32,128]{2,1,0:T(8,128)(2,1)}), bf16[128,32,128]{2,1,0:T(8,128)(2,1)S(1)}, u32[]{:S(2)}, u32[]{:S(2)}) async-start(bf16[128,32,128]{2,1,0:T(8,128)(2,1)} %bitcast.18), calls=%async_computation | async-start | bytes 2097152 | tf_op jit(solution)/shard_map/all_to_all | solution.py:591
  17.1 1.4 %copy-start = (bf16[512,1536]{1,0:T(8,128)(2,1)S(1)}, bf16[512,1536]{1,0:T(8,128)(2,1)}, u32[]{:S(2)}) copy-start(bf16[512,1536]{1,0:T(8,128)(2,1)} %state_hbm.1) | copy-start | bytes 4718596
  18.5 1.4 %copy-start.1 = (bf16[512,1536]{1,0:T(8,128)(2,1)S(1)}, bf16[512,1536]{1,0:T(8,128)(2,1)}, u32[]{:S(2)}) copy-start(bf16[512,1536]{1,0:T(8,128)(2,1)} %input_hbm.1) | copy-start | bytes 4718596
  20.0 1.1 %copy-start.2 = (f32[12,8,4,512]{3,2,1,0:T(4,128)S(1)}, f32[12,8,4,512]{3,2,1,0:T(4,128)}, u32[]{:S(2)}) copy-start(f32[12,8,4,512]{3,2,1,0:T(4,128)} %hidden_hbm.1) | copy-start | bytes 2359300
  21.1 1.0 %copy-start.3 = (bf16[256,1024]{1,0:T(8,128)(2,1)S(1)}, bf16[256,1024]{1,0:T(8,128)(2,1)}, u32[]{:S(2)}) copy-start(bf16[256,1024]{1,0:T(8,128)(2,1)} %expand_hbm.1) | copy-start | bytes 1572868
  22.1 1.0 %copy-start.4 = (bf16[1024,256]{1,0:T(8,128)(2,1)S(1)}, bf16[1024,256]{1,0:T(8,128)(2,1)}, u32[]{:S(2)}) copy-start(bf16[1024,256]{1,0:T(8,128)(2,1)} %reduce_hbm.1) | copy-start | bytes 1572868
  23.2 0.9 %copy-start.5 = (bf16[256,512]{1,0:T(8,128)(2,1)S(1)}, bf16[256,512]{1,0:T(8,128)(2,1)}, u32[]{:S(2)}) copy-start(bf16[256,512]{1,0:T(8,128)(2,1)} %project_hbm.1) | copy-start | bytes 786436

commit v4 on v3

--- a/solution.py
+++ b/solution.py
@@ -13,9 +13,11 @@
 DEPTH = (KERNEL + 1) * SIDE
 
 VMEM_LIMIT = 63 * 1024 * 1024
+READY_VMEM = 52 * 1024 * 1024
 RECEIVE_VMEM = 44 * 1024 * 1024
 WEIGHT_ROWS = 8192
 STATE_FACES = 34 * FACES
+STATE_ROWS = 4096
 
 f32 = jnp.float32
 bf16 = jnp.bfloat16
@@ -279,14 +281,15 @@
 def receive_kernel(
     msg_ref,
     vector_ref,
-    from_state_ref,
-    weight_hbm,
-    held_hbm,
-    out_hbm,
     expand_ref,
     reduce_ref,
     project_ref,
+    weight_hbm,
+    state_hbm,
+    held_hbm,
+    out_hbm,
     input_ref,
+    from_state_ref,
     hidden_ref,
     out_ref,
     wide_ref,
@@ -297,10 +300,8 @@
     out_sem,
 ):
     operands = [
-        (expand_part(weight_hbm), expand_ref),
-        (reduce_part(weight_hbm), reduce_ref),
-        (project_part(weight_hbm), project_ref),
-        (input_part(weight_hbm), input_ref),
+        (weight_hbm.at[pl.ds(0, 512)], input_ref),
+        (state_hbm.at[pl.ds(0, 384)], from_state_ref),
         (held_hbm.at[pl.ds(0, FACES)], hidden_ref),
     ]
     loads = [
@@ -335,7 +336,6 @@
         normed_ref[di * 2 + 1, rows, :] = cells[48:96]
         pooled_ref[ci * 48 + di * 24 : ci * 48 + (di + 1) * 24, :] = cells[96:].astype(f32)[:24]
 
-    loads[0].wait()
     for k in range(4):
         lanes = slice(k * 256, (k + 1) * 256)
         for m in range(3):
@@ -352,8 +352,6 @@
                 total = unit if total is None else total + unit
             units_ref[rows, lanes] = total.astype(bf16)
 
-    loads[1].wait()
-    loads[2].wait()
     update = (
         jnp.dot(units_ref[...], reduce_ref[...], preferred_element_type=f32) * 0.125
         + vector(1, slice(0, 256))
@@ -363,12 +361,13 @@
         jnp.dot(pooled, project_ref[...], preferred_element_type=f32) + vector(3, slice(0, 512))
     ).astype(bf16)
 
-    for copy in loads[3:]:
+    for copy in loads:
         copy.wait()
 
     def sigmoid(v):
         return 0.5 * jnp.tanh(0.5 * v) + 0.5
 
+    sends = []
     for k in range(2):
 
         def gate(block):
@@ -393,25 +392,14 @@
                 out_ref[f, ci, :, lanes] = kept + update_gate[rows] * (
                     hidden_ref[f, ci, :, lanes] - kept
                 )
-    copy = pltpu.make_async_copy(out_ref, out_hbm, out_sem)
-    copy.start()
-    copy.wait()
-
-
-def input_part(ref):
-    return ref.at[pl.ds(0, 512)]
-
-
-def expand_part(ref):
-    return ref.at[pl.ds(512, 256), pl.ds(0, 1024)]
-
-
-def project_part(ref):
-    return ref.at[pl.ds(512, 256), pl.ds(1024, 512)]
-
-
-def reduce_part(ref):
-    return ref.at[pl.ds(768, 1024), pl.ds(0, 256)]
+        sends.append(
+            pltpu.make_async_copy(
+                out_ref.at[:, :, :, lanes], out_hbm.at[:, :, :, lanes], out_sem.at[k]
+            )
+        )
+        sends[-1].start()
+    for copy in sends:
+        copy.wait()
 
 
 def ready_kernel(
@@ -429,9 +417,12 @@
     reduce_hbm,
     project_hbm,
     input_hbm,
-    from_state_ref,
     vector_ref,
+    expand_ref,
+    reduce_ref,
+    project_ref,
     weight_hbm,
+    state_part_hbm,
     held_hbm,
     hidden_ref,
     state_ref,
@@ -444,6 +435,8 @@
     project_bias_ref,
     input_bias_ref,
     previous_ref,
+    from_state_ref,
+    input_ref,
     sems,
     pack_sems,
 ):
@@ -451,11 +444,10 @@
         pltpu.make_async_copy(source, target, pack_sems.at[k])
         for k, (source, target) in enumerate(
             [
-                (expand_hbm, expand_part(weight_hbm)),
-                (reduce_hbm, reduce_part(weight_hbm)),
-                (project_hbm, project_part(weight_hbm)),
-                (input_hbm, input_part(weight_hbm)),
-                (hidden_hbm, held_hbm.at[pl.ds(0, FACES)]),
+                (expand_hbm, expand_ref),
+                (reduce_hbm, reduce_ref),
+                (project_hbm, project_ref),
+                (input_hbm, input_ref),
             ]
         )
     ]
@@ -479,8 +471,19 @@
     ]
     for copy in loads:
         copy.start()
-    for copy in loads:
+    for copy in loads + packs:
         copy.wait()
+    packs = [
+        pltpu.make_async_copy(source, target, pack_sems.at[4 + k])
+        for k, (source, target) in enumerate(
+            [
+                (input_ref, weight_hbm.at[pl.ds(0, 512)]),
+                (hidden_ref, held_hbm.at[pl.ds(0, FACES)]),
+            ]
+        )
+    ]
+    for copy in packs:
+        copy.start()
     for ci in range(8):
         for f in range(FACES):
             at = ci * 48 + f * 4
@@ -493,6 +496,12 @@
             )
             + state_bias_ref[:, lanes]
         )
+    packs.append(
+        pltpu.make_async_copy(
+            from_state_ref, state_part_hbm.at[pl.ds(0, 384)], pack_sems.at[6]
+        )
+    )
+    packs[-1].start()
     vectors = (
         expand_bias_ref,
         reduce_bias_ref,
@@ -515,54 +524,55 @@
     return pl.pallas_call(
         ready_kernel,
         out_shape=(
-            jax.ShapeDtypeStruct((384, 1536), f32),
             jax.ShapeDtypeStruct((8, 1536), f32),
+            *(jax.ShapeDtypeStruct(v.shape, v.dtype) for v in weights[:3]),
             jax.ShapeDtypeStruct((WEIGHT_ROWS, 1536), bf16),
+            jax.ShapeDtypeStruct((STATE_ROWS, 1536), f32),
             jax.ShapeDtypeStruct((STATE_FACES, 8, 4, 512), f32),
         ),
         in_specs=[hbm] * (len(operands) + len(weights)),
-        out_specs=(vmem, vmem, hbm, hbm),
+        out_specs=(vmem,) * 4 + (hbm,) * 3,
         scratch_shapes=[pltpu.VMEM(v.shape, v.dtype) for v in operands]
         + [
             pltpu.VMEM((384, 512), f32),
+            pltpu.VMEM((384, 1536), f32),
+            pltpu.VMEM((512, 1536), bf16),
             pltpu.SemaphoreType.DMA((len(operands),)),
-            pltpu.SemaphoreType.DMA((5,)),
+            pltpu.SemaphoreType.DMA((7,)),
         ],
         cost_estimate=pl.CostEstimate(
             flops=2 * 384 * 512 * 1536, bytes_accessed=8000000, transcendentals=0
         ),
-        compiler_params=pltpu.CompilerParams(vmem_limit_bytes=RECEIVE_VMEM),
+        compiler_params=pltpu.CompilerParams(vmem_limit_bytes=READY_VMEM),
     )(*operands, *weights)
 
 
-def receive(message, vectors, from_state, weights, held):
+def receive(*operands):
     vmem = pl.BlockSpec(memory_space=pltpu.VMEM)
     hbm = pl.BlockSpec(memory_space=pl.ANY)
     result = jax.ShapeDtypeStruct((FACES, 8, 4, 512), f32)
     return pl.pallas_call(
         receive_kernel,
         out_shape=result,
-        in_specs=[vmem, vmem, vmem, hbm, hbm],
+        in_specs=[vmem] * 5 + [hbm] * 3,
         out_specs=hbm,
         scratch_shapes=[
-            pltpu.VMEM((256, 1024), bf16),
-            pltpu.VMEM((1024, 256), bf16),
-            pltpu.VMEM((256, 512), bf16),
             pltpu.VMEM((512, 1536), bf16),
+            pltpu.VMEM((384, 1536), f32),
             pltpu.VMEM(result.shape, f32),
             pltpu.VMEM(result.shape, f32),
             pltpu.VMEM((4096, SIDE), f32),
             pltpu.VMEM((4, 384, 256), bf16),
             pltpu.VMEM((384, 256), f32),
             pltpu.VMEM((384, 1024), bf16),
-            pltpu.SemaphoreType.DMA((5,)),
-            pltpu.SemaphoreType.DMA,
+            pltpu.SemaphoreType.DMA((3,)),
+            pltpu.SemaphoreType.DMA((2,)),
         ],
         cost_estimate=pl.CostEstimate(
             flops=2 * 700000000, bytes_accessed=8000000, transcendentals=2000000
         ),
         compiler_params=pltpu.CompilerParams(vmem_limit_bytes=RECEIVE_VMEM),
-    )(message, vectors, from_state, weights, held)
+    )(*operands)
 
 
 def shards(
@@ -589,7 +599,7 @@
     message = send(features, conv_kernel, conv_bias, neighbour_face, neighbour_side)
     message = message.reshape(128, 32, SIDE)
     arrived = lax.all_to_all(message, ("ty", "tx"), split_axis=0, concat_axis=0, tiled=True)
-    from_state, vectors, weights, held = ready(
+    operands = ready(
         hidden_state,
         state_gates,
         (
@@ -604,7 +614,7 @@
         ),
         (expand_weight, reduce_weight, project_weight, input_gates),
     )
-    return receive(arrived.reshape(4096, SIDE), vectors, from_state, weights, held)
+    return receive(arrived.reshape(4096, SIDE), *operands)
 
 
 def solution(mesh):

time: 42.3 us -> 41.6 us (0.983)
  waiting for transfers between devices: 10 us -> 7.76 us
  Pallas kernels: 13.2 us -> 15.4 us
  local copies, waits for them, and re-layouts: 7.02 us -> 6.44 us
    pallas_call x2, Pallas kernels: 7.71 us -> 10 us  [the longest x1 5.16 us: receive(): pl.pallas_call(receive_kernel, out_shape=result, in_specs=[vmem] * 5 + [h...]
    all_to_all x1, waiting for transfers between devices: 10 us -> 7.76 us  [shards(): lax.all_to_all(message, ('ty', 'tx'), split_axis=0, concat_axis=0, tiled=...]
    unnamed x28 -> x14, local copies, waits for them, and re-layouts: 7.01 us -> 5.03 us
    reshape x2, local copies, waits for them, and re-layouts: 0.01 us -> 1.41 us  [ready(): v.reshape(1, -1)]
  transfers between devices with their start and end apart: 1 -> 1, of which waited for: 1 -> 1; matrix products, arithmetic and copies ran while one was open for 0% -> 3% of each run, Pallas kernels for 5% -> 12%
where the time goes in v4:
time: 41.6 us; the launch traced here: 41.1 us
  Pallas kernels  15.4 us (37%)
  starting transfers between devices  11.5 us (28%)
  waiting for transfers between devices  7.76 us (19%)
  local copies, waits for them, and re-layouts  6.44 us (15%)
    all_to_all x1, starting transfers between devices, shards(): lax.all_to_all(message, ('ty', 'tx'), split_axis=0, concat_axis=0, tiled=...  11.5 us
    all_to_all x1, waiting for transfers between devices, shards(): lax.all_to_all(message, ('ty', 'tx'), split_axis=0, concat_axis=0, tiled=...  7.76 us
    pallas_call x1, Pallas kernels, send(): pl.pallas_call(send_kernel, out_shape=jax.ShapeDtypeStruct((8, 16, 32, SI...  5.39 us
    pallas_call x1, Pallas kernels, receive(): pl.pallas_call(receive_kernel, out_shape=result, in_specs=[vmem] * 5 + [h...  5.16 us
    unnamed x14, local copies, waits for them, and re-layouts  5.03 us
    pallas_call x1, Pallas kernels, ready(): pl.pallas_call(ready_kernel, out_shape=(jax.ShapeDtypeStruct((8, 1536), f...  4.85 us
    reshape x2, local copies, waits for them, and re-layouts, ready(): v.reshape(1, -1)  1.41 us
  transfers between devices with their start and end apart: 1, of which 1 were waited for; matrix products, arithmetic and copies ran while one was open for 3% of the time, Pallas kernels for 12%

profile of v4, /device:TPU:1, one launch (start us, length us, event | category | flops | bytes accessed | tf_op | source)
XLA Modules:
  0.0 41.1 jit_solution(8899771921708801604)
XLA Ops:
  0.0 5.4 %shard_map.181 = bf16[8,16,32,128]{3,2,1,0:T(8,128)(2,1)} custom-call(f32[2,49]{1,0:T(2,128)} %bitcast.21, s32[4,12]{1,0:T(4,128)} %bitcast.19, s32[4,12]{1,0:T(4,128)} %bitcast.20, f32[2]{0:T(128)} %bias_hbm.1, bf16[2,12,128,128]{3,2,1,0:T(8,128)(2,1)} %x_hbm.1), custom_call_target="tpu_custom_call" | custom-call | flops 1610612736 | bytes 4000000 | tf_op jit(solution)/shard_map/pallas_call | solution.py:251
  5.4 11.5 %all-to-all-start = ((bf16[128,32,128]{2,1,0:T(8,128)(2,1)}), bf16[128,32,128]{2,1,0:T(8,128)(2,1)S(1)}, u32[]{:S(2)}, u32[]{:S(2)}) async-start(bf16[128,32,128]{2,1,0:T(8,128)(2,1)} %bitcast.18), calls=%async_computation | async-start | bytes 2097152 | tf_op jit(solution)/shard_map/all_to_all | solution.py:601
  16.9 0.7 %reshape.39.input_bias_hbm = f32[1,1536]{1,0:T(1,128)S(1)} reshape(f32[1536]{0:T(1024)} %param.34) | data formatting | bytes 12288 | tf_op jit(solution)/shard_map/reshape | solution.py:523
  17.6 0.7 %reshape.32.state_bias_hbm = f32[1,1536]{1,0:T(1,128)S(1)} reshape(f32[1536]{0:T(1024)} %param.36) | data formatting | bytes 12288 | tf_op jit(solution)/shard_map/reshape | solution.py:523
  18.3 0.0 copy-start
  18.3 0.9 %copy-done = bf16[256,512]{1,0:T(8,128)(2,1)S(1)} copy-done((bf16[256,512]{1,0:T(8,128)(2,1)S(1)}, bf16[256,512]{1,0:T(8,128)(2,1)}, u32[]{:S(2)}) %copy-start) | copy-done | bytes 262168
  19.3 0.0 copy-start.1
  19.3 0.7 %copy-done.1 = f32[1024]{0:T(1024)S(1)} copy-done((f32[1024]{0:T(1024)S(1)}, f32[1024]{0:T(1024)}, u32[]{:S(2)}) %copy-start.1) | copy-done | bytes 4120
  20.0 0.0 copy-start.2
  20.0 0.7 %copy-done.2 = f32[512]{0:T(512)S(1)} copy-done((f32[512]{0:T(512)S(1)}, f32[512]{0:T(512)}, u32[]{:S(2)}) %copy-start.2) | copy-done | bytes 2072
  20.6 0.0 copy-start.3
  20.6 0.7 %copy-done.3 = f32[256]{0:T(256)S(1)} copy-done((f32[256]{0:T(256)S(1)}, f32[256]{0:T(256)}, u32[]{:S(2)}) %copy-start.3) | copy-done | bytes 1048
  21.3 0.0 copy-start.4
  21.3 0.7 %copy-done.4 = f32[256]{0:T(256)S(1)} copy-done((f32[256]{0:T(256)S(1)}, f32[256]{0:T(256)}, u32[]{:S(2)}) %copy-start.4) | copy-done | bytes 1048
  22.0 0.0 copy-start.5
  22.0 0.7 %copy-done.5 = f32[256]{0:T(256)S(1)} copy-done((f32[256]{0:T(256)S(1)}, f32[256]{0:T(256)}, u32[]{:S(2)}) %copy-start.5) | copy-done | bytes 1048
  22.7 0.0 copy-start.6
  22.7 0.7 %copy-done.6 = f32[256]{0:T(256)S(1)} copy-done((f32[256]{0:T(256)S(1)}, f32[256]{0:T(256)}, u32[]{:S(2)}) %copy-start.6) | copy-done | bytes 1048
  23.4 4.8 %shard_map.182 = (f32[8,1536]{1,0:T(8,128)S(1)}, bf16[256,1024]{1,0:T(8,128)(2,1)S(1)}, bf16[1024,256]{1,0:T(8,128)(2,1)S(1)}, bf16[256,512]{1,0:T(8,128)(2,1)S(...) custom-call(f32[12,8,4,512]{3,2,1,0:T(4,128)} %hidden_hbm.1, ...), custom_call_target="tpu_custom_call" | custom-call | flops 603979776 | bytes 8000000 | tf_op jit(solution)/shard_map/pallas_call | solution.py:524
  28.2 7.8 %all-to-all-done = bf16[128,32,128]{2,1,0:T(8,128)(2,1)S(1)} async-done(((bf16[128,32,128]{2,1,0:T(8,128)(2,1)}), bf16[128,32,128]{2,1,0:T(8,128)(2,1)S(1)}, u32[]{:S(2)}, u32[]{:S(2)}) %all-to-all-start) | async-done | bytes 1048608 | tf_op jit(solution)/shard_map/all_to_all | solution.py:601
  36.0 5.2 %shard_map.183 = f32[12,8,4,512]{3,2,1,0:T(4,128)} custom-call(bf16[4096,128]{1,0:T(8,128)(2,1)S(1)} %bitcast.11, f32[8,1536]{1,0:T(8,128)S(1)} %get-tuple-element.12.vector_ref, bf16[256,1024]{1,0:T(8,128)(2,1)S(1)} %get-tuple-element.13.expand_ref, bf16[1024,256]{1,0:T(8,128)(2,1)S(1)} %get-tuple-element.14.reduce_ref, ...), custom_call_target="tpu_custom_call" | custom-call | flops 1400000000 | bytes 8000000 | tf_op jit(solution)/shard_map/pallas_call | solution.py:554
Async XLA Ops:
  5.4 30.6 %all-to-all-start = ((bf16[128,32,128]{2,1,0:T(8,128)(2,1)}), bf16[128,32,128]{2,1,0:T(8,128)(2,1)S(1)}, u32[]{:S(2)}, u32[]{:S(2)}) async-start(bf16[128,32,128]{2,1,0:T(8,128)(2,1)} %bitcast.18), calls=%async_computation | async-start | bytes 2097152 | tf_op jit(solution)/shard_map/all_to_all | solution.py:601
  18.3 0.9 %copy-start = (bf16[256,512]{1,0:T(8,128)(2,1)S(1)}, bf16[256,512]{1,0:T(8,128)(2,1)}, u32[]{:S(2)}) copy-start(bf16[256,512]{1,0:T(8,128)(2,1)} %project_hbm.1) | copy-start | bytes 786436
  19.3 0.7 %copy-start.1 = (f32[1024]{0:T(1024)S(1)}, f32[1024]{0:T(1024)}, u32[]{:S(2)}) copy-start(f32[1024]{0:T(1024)} %param.27) | copy-start | bytes 12292
  20.0 0.7 %copy-start.2 = (f32[512]{0:T(512)S(1)}, f32[512]{0:T(512)}, u32[]{:S(2)}) copy-start(f32[512]{0:T(512)} %param.32) | copy-start | bytes 6148
  20.6 0.7 %copy-start.3 = (f32[256]{0:T(256)S(1)}, f32[256]{0:T(256)}, u32[]{:S(2)}) copy-start(f32[256]{0:T(256)} %param.24) | copy-start | bytes 3076
  21.3 0.7 %copy-start.4 = (f32[256]{0:T(256)S(1)}, f32[256]{0:T(256)}, u32[]{:S(2)}) copy-start(f32[256]{0:T(256)} %param.25) | copy-start | bytes 3076
  22.0 0.7 %copy-start.5 = (f32[256]{0:T(256)S(1)}, f32[256]{0:T(256)}, u32[]{:S(2)}) copy-start(f32[256]{0:T(256)} %param.29) | copy-start | bytes 3076
  22.7 0.7 %copy-start.6 = (f32[256]{0:T(256)S(1)}, f32[256]{0:T(256)}, u32[]{:S(2)}) copy-start(f32[256]{0:T(256)} %param.30) | copy-start | bytes 3076

commit v5 on v4

--- a/solution.py
+++ b/solution.py
@@ -106,14 +106,13 @@
     band = jnp.where(row8 < 4, 2 - row8 - head, SIDE + 3 + (row8 - 4) - head)
     band = jnp.where((row8 & 3) == 3, -1, band)
 
-    for copy in loads:
-        copy.wait()
-
     def store_weights(c, rows, value):
         high = value.astype(bf16)
         rhs_ref[c, rows, :SIDE] = high
         rhs_ref[c, rows, SIDE:] = (value - high.astype(f32)).astype(bf16)
 
+    for copy in loads[:4]:
+        copy.wait()
     for c in range(2):
         borders = []
         for q in range(KERNEL):
@@ -135,6 +134,9 @@
         borders.append(jnp.zeros((SIDE - 8 * KERNEL, SIDE), f32))
         store_weights(c, slice(KERNEL * SIDE, DEPTH), jnp.concatenate(borders, axis=0))
 
+    for copy in loads[4:]:
+        copy.wait()
+    sends = []
     for c in range(2):
 
         def prepare(f, c=c):
@@ -153,9 +155,6 @@
 
         for f in range(FACES):
             prepare(f)
-
-    sends = []
-    for c in range(2):
 
         def assemble(f, c=c):
             at = [face_ref[s, f] * 4 + side_ref[s, f] for s in range(4)]

time: 41.6 us -> 41.2 us (level)
  no operation moved by 1% of the time
where the time goes in v5:
time: 41.2 us; the launch traced here: 40.8 us
  Pallas kernels  15.1 us (37%)
  starting transfers between devices  11.5 us (28%)
  waiting for transfers between devices  7.77 us (19%)
  local copies, waits for them, and re-layouts  6.44 us (16%)
    all_to_all x1, starting transfers between devices, shards(): lax.all_to_all(message, ('ty', 'tx'), split_axis=0, concat_axis=0, tiled=...  11.5 us
    all_to_all x1, waiting for transfers between devices, shards(): lax.all_to_all(message, ('ty', 'tx'), split_axis=0, concat_axis=0, tiled=...  7.77 us
    pallas_call x1, Pallas kernels, receive(): pl.pallas_call(receive_kernel, out_shape=result, in_specs=[vmem] * 5 + [h...  5.15 us
    pallas_call x1, Pallas kernels, send(): pl.pallas_call(send_kernel, out_shape=jax.ShapeDtypeStruct((8, 16, 32, SI...  5.06 us
    unnamed x14, local copies, waits for them, and re-layouts  5.03 us
    pallas_call x1, Pallas kernels, ready(): pl.pallas_call(ready_kernel, out_shape=(jax.ShapeDtypeStruct((8, 1536), f...  4.84 us
    reshape x2, local copies, waits for them, and re-layouts, ready(): v.reshape(1, -1)  1.41 us
  transfers between devices with their start and end apart: 1, of which 1 were waited for; matrix products, arithmetic and copies ran while one was open for 3% of the time, Pallas kernels for 12%

profile of v5, /device:TPU:1, one launch (start us, length us, event | category | flops | bytes accessed | tf_op | source)
XLA Modules:
  0.0 40.8 jit_solution(74137308517986830)
XLA Ops:
  0.0 5.1 %shard_map.181 = bf16[8,16,32,128]{3,2,1,0:T(8,128)(2,1)} custom-call(f32[2,49]{1,0:T(2,128)} %bitcast.21, s32[4,12]{1,0:T(4,128)} %bitcast.19, s32[4,12]{1,0:T(4,128)} %bitcast.20, f32[2]{0:T(128)} %bias_hbm.1, bf16[2,12,128,128]{3,2,1,0:T(8,128)(2,1)} %x_hbm.1), custom_call_target="tpu_custom_call" | custom-call | flops 1610612736 | bytes 4000000 | tf_op jit(solution)/shard_map/pallas_call | solution.py:250
  5.1 11.5 %all-to-all-start = ((bf16[128,32,128]{2,1,0:T(8,128)(2,1)}), bf16[128,32,128]{2,1,0:T(8,128)(2,1)S(1)}, u32[]{:S(2)}, u32[]{:S(2)}) async-start(bf16[128,32,128]{2,1,0:T(8,128)(2,1)} %bitcast.18), calls=%async_computation | async-start | bytes 2097152 | tf_op jit(solution)/shard_map/all_to_all | solution.py:600
  16.6 0.7 %reshape.39.input_bias_hbm = f32[1,1536]{1,0:T(1,128)S(1)} reshape(f32[1536]{0:T(1024)} %param.34) | data formatting | bytes 12288 | tf_op jit(solution)/shard_map/reshape | solution.py:522
  17.3 0.7 %reshape.32.state_bias_hbm = f32[1,1536]{1,0:T(1,128)S(1)} reshape(f32[1536]{0:T(1024)} %param.36) | data formatting | bytes 12288 | tf_op jit(solution)/shard_map/reshape | solution.py:522
  18.0 0.0 copy-start
  18.0 0.9 %copy-done = bf16[256,512]{1,0:T(8,128)(2,1)S(1)} copy-done((bf16[256,512]{1,0:T(8,128)(2,1)S(1)}, bf16[256,512]{1,0:T(8,128)(2,1)}, u32[]{:S(2)}) %copy-start) | copy-done | bytes 262168
  18.9 0.0 copy-start.1
  18.9 0.7 %copy-done.1 = f32[1024]{0:T(1024)S(1)} copy-done((f32[1024]{0:T(1024)S(1)}, f32[1024]{0:T(1024)}, u32[]{:S(2)}) %copy-start.1) | copy-done | bytes 4120
  19.6 0.0 copy-start.2
  19.6 0.7 %copy-done.2 = f32[512]{0:T(512)S(1)} copy-done((f32[512]{0:T(512)S(1)}, f32[512]{0:T(512)}, u32[]{:S(2)}) %copy-start.2) | copy-done | bytes 2072
  20.3 0.0 copy-start.3
  20.3 0.7 %copy-done.3 = f32[256]{0:T(256)S(1)} copy-done((f32[256]{0:T(256)S(1)}, f32[256]{0:T(256)}, u32[]{:S(2)}) %copy-start.3) | copy-done | bytes 1048
  21.0 0.0 copy-start.4
  21.0 0.7 %copy-done.4 = f32[256]{0:T(256)S(1)} copy-done((f32[256]{0:T(256)S(1)}, f32[256]{0:T(256)}, u32[]{:S(2)}) %copy-start.4) | copy-done | bytes 1048
  21.7 0.0 copy-start.5
  21.7 0.7 %copy-done.5 = f32[256]{0:T(256)S(1)} copy-done((f32[256]{0:T(256)S(1)}, f32[256]{0:T(256)}, u32[]{:S(2)}) %copy-start.5) | copy-done | bytes 1048
  22.4 0.0 copy-start.6
  22.4 0.7 %copy-done.6 = f32[256]{0:T(256)S(1)} copy-done((f32[256]{0:T(256)S(1)}, f32[256]{0:T(256)}, u32[]{:S(2)}) %copy-start.6) | copy-done | bytes 1048
  23.0 4.8 %shard_map.182 = (f32[8,1536]{1,0:T(8,128)S(1)}, bf16[256,1024]{1,0:T(8,128)(2,1)S(1)}, bf16[1024,256]{1,0:T(8,128)(2,1)S(1)}, bf16[256,512]{1,0:T(8,128)(2,1)S(...) custom-call(f32[12,8,4,512]{3,2,1,0:T(4,128)} %hidden_hbm.1, ...), custom_call_target="tpu_custom_call" | custom-call | flops 603979776 | bytes 8000000 | tf_op jit(solution)/shard_map/pallas_call | solution.py:523
  27.9 7.8 %all-to-all-done = bf16[128,32,128]{2,1,0:T(8,128)(2,1)S(1)} async-done(((bf16[128,32,128]{2,1,0:T(8,128)(2,1)}), bf16[128,32,128]{2,1,0:T(8,128)(2,1)S(1)}, u32[]{:S(2)}, u32[]{:S(2)}) %all-to-all-start) | async-done | bytes 1048608 | tf_op jit(solution)/shard_map/all_to_all | solution.py:600
  35.7 5.2 %shard_map.183 = f32[12,8,4,512]{3,2,1,0:T(4,128)} custom-call(bf16[4096,128]{1,0:T(8,128)(2,1)S(1)} %bitcast.11, f32[8,1536]{1,0:T(8,128)S(1)} %get-tuple-element.12.vector_ref, bf16[256,1024]{1,0:T(8,128)(2,1)S(1)} %get-tuple-element.13.expand_ref, bf16[1024,256]{1,0:T(8,128)(2,1)S(1)} %get-tuple-element.14.reduce_ref, ...), custom_call_target="tpu_custom_call" | custom-call | flops 1400000000 | bytes 8000000 | tf_op jit(solution)/shard_map/pallas_call | solution.py:553
Async XLA Ops:
  5.1 30.6 %all-to-all-start = ((bf16[128,32,128]{2,1,0:T(8,128)(2,1)}), bf16[128,32,128]{2,1,0:T(8,128)(2,1)S(1)}, u32[]{:S(2)}, u32[]{:S(2)}) async-start(bf16[128,32,128]{2,1,0:T(8,128)(2,1)} %bitcast.18), calls=%async_computation | async-start | bytes 2097152 | tf_op jit(solution)/shard_map/all_to_all | solution.py:600
  18.0 0.9 %copy-start = (bf16[256,512]{1,0:T(8,128)(2,1)S(1)}, bf16[256,512]{1,0:T(8,128)(2,1)}, u32[]{:S(2)}) copy-start(bf16[256,512]{1,0:T(8,128)(2,1)} %project_hbm.1) | copy-start | bytes 786436
  18.9 0.7 %copy-start.1 = (f32[1024]{0:T(1024)S(1)}, f32[1024]{0:T(1024)}, u32[]{:S(2)}) copy-start(f32[1024]{0:T(1024)} %param.27) | copy-start | bytes 12292
  19.6 0.7 %copy-start.2 = (f32[512]{0:T(512)S(1)}, f32[512]{0:T(512)}, u32[]{:S(2)}) copy-start(f32[512]{0:T(512)} %param.32) | copy-start | bytes 6148
  20.3 0.7 %copy-start.3 = (f32[256]{0:T(256)S(1)}, f32[256]{0:T(256)}, u32[]{:S(2)}) copy-start(f32[256]{0:T(256)} %param.24) | copy-start | bytes 3076
  21.0 0.7 %copy-start.4 = (f32[256]{0:T(256)S(1)}, f32[256]{0:T(256)}, u32[]{:S(2)}) copy-start(f32[256]{0:T(256)} %param.25) | copy-start | bytes 3076
  21.7 0.7 %copy-start.5 = (f32[256]{0:T(256)S(1)}, f32[256]{0:T(256)}, u32[]{:S(2)}) copy-start(f32[256]{0:T(256)} %param.29) | copy-start | bytes 3076
  22.4 0.7 %copy-start.6 = (f32[256]{0:T(256)S(1)}, f32[256]{0:T(256)}, u32[]{:S(2)}) copy-start(f32[256]{0:T(256)} %param.30) | copy-start | bytes 3076

commit v6 on v5

--- a/solution.py
+++ b/solution.py
@@ -85,7 +85,7 @@
             ]
         )
     ] + [pltpu.make_async_copy(x_hbm.at[c], x_ref.at[c], x_sem.at[c]) for c in range(2)]
-    for copy in loads:
+    for copy in loads[4:] + loads[:4]:
         copy.start()
 
     i = iota((SIDE, SIDE), 0)
@@ -347,7 +347,7 @@
             total = None
             for s in range(4):
                 part = hidden[s * 128 : (s + 1) * 128] + vector(0, lanes)
-                unit = part * (1.0 + lax.erf(part * (0.5**0.5)))
+                unit = part + part * lax.erf(part * (0.5**0.5))
                 total = unit if total is None else total + unit
             units_ref[rows, lanes] = total.astype(bf16)
 

time: 41.2 us -> 41.2 us (level)
  no operation moved by 1% of the time
where the time goes in v6:
time: 41.2 us; the launch traced here: 40.8 us
  Pallas kernels  15 us (36%)
  starting transfers between devices  11.5 us (28%)
  waiting for transfers between devices  7.77 us (19%)
  local copies, waits for them, and re-layouts  6.44 us (16%)
    all_to_all x1, starting transfers between devices, shards(): lax.all_to_all(message, ('ty', 'tx'), split_axis=0, concat_axis=0, tiled=...  11.5 us
    all_to_all x1, waiting for transfers between devices, shards(): lax.all_to_all(message, ('ty', 'tx'), split_axis=0, concat_axis=0, tiled=...  7.77 us
    pallas_call x1, Pallas kernels, receive(): pl.pallas_call(receive_kernel, out_shape=result, in_specs=[vmem] * 5 + [h...  5.13 us
    pallas_call x1, Pallas kernels, send(): pl.pallas_call(send_kernel, out_shape=jax.ShapeDtypeStruct((8, 16, 32, SI...  5.07 us
    unnamed x14, local copies, waits for them, and re-layouts  5.03 us
    pallas_call x1, Pallas kernels, ready(): pl.pallas_call(ready_kernel, out_shape=(jax.ShapeDtypeStruct((8, 1536), f...  4.84 us
    reshape x2, local copies, waits for them, and re-layouts, ready(): v.reshape(1, -1)  1.41 us
  transfers between devices with their start and end apart: 1, of which 1 were waited for; matrix products, arithmetic and copies ran while one was open for 3% of the time, Pallas kernels for 12%

profile of v6, /device:TPU:1, one launch (start us, length us, event | category | flops | bytes accessed | tf_op | source)
XLA Modules:
  0.0 40.8 jit_solution(2282355942964238595)
XLA Ops:
  0.0 5.1 %shard_map.181 = bf16[8,16,32,128]{3,2,1,0:T(8,128)(2,1)} custom-call(f32[2,49]{1,0:T(2,128)} %bitcast.21, s32[4,12]{1,0:T(4,128)} %bitcast.19, s32[4,12]{1,0:T(4,128)} %bitcast.20, f32[2]{0:T(128)} %bias_hbm.1, bf16[2,12,128,128]{3,2,1,0:T(8,128)(2,1)} %x_hbm.1), custom_call_target="tpu_custom_call" | custom-call | flops 1610612736 | bytes 4000000 | tf_op jit(solution)/shard_map/pallas_call | solution.py:250
  5.1 11.5 %all-to-all-start = ((bf16[128,32,128]{2,1,0:T(8,128)(2,1)}), bf16[128,32,128]{2,1,0:T(8,128)(2,1)S(1)}, u32[]{:S(2)}, u32[]{:S(2)}) async-start(bf16[128,32,128]{2,1,0:T(8,128)(2,1)} %bitcast.18), calls=%async_computation | async-start | bytes 2097152 | tf_op jit(solution)/shard_map/all_to_all | solution.py:600
  16.6 0.7 %reshape.39.input_bias_hbm = f32[1,1536]{1,0:T(1,128)S(1)} reshape(f32[1536]{0:T(1024)} %param.34) | data formatting | bytes 12288 | tf_op jit(solution)/shard_map/reshape | solution.py:522
  17.3 0.7 %reshape.32.state_bias_hbm = f32[1,1536]{1,0:T(1,128)S(1)} reshape(f32[1536]{0:T(1024)} %param.36) | data formatting | bytes 12288 | tf_op jit(solution)/shard_map/reshape | solution.py:522
  18.0 0.0 copy-start
  18.0 0.9 %copy-done = bf16[256,512]{1,0:T(8,128)(2,1)S(1)} copy-done((bf16[256,512]{1,0:T(8,128)(2,1)S(1)}, bf16[256,512]{1,0:T(8,128)(2,1)}, u32[]{:S(2)}) %copy-start) | copy-done | bytes 262168
  18.9 0.0 copy-start.1
  18.9 0.7 %copy-done.1 = f32[1024]{0:T(1024)S(1)} copy-done((f32[1024]{0:T(1024)S(1)}, f32[1024]{0:T(1024)}, u32[]{:S(2)}) %copy-start.1) | copy-done | bytes 4120
  19.6 0.0 copy-start.2
  19.6 0.7 %copy-done.2 = f32[512]{0:T(512)S(1)} copy-done((f32[512]{0:T(512)S(1)}, f32[512]{0:T(512)}, u32[]{:S(2)}) %copy-start.2) | copy-done | bytes 2072
  20.3 0.0 copy-start.3
  20.3 0.7 %copy-done.3 = f32[256]{0:T(256)S(1)} copy-done((f32[256]{0:T(256)S(1)}, f32[256]{0:T(256)}, u32[]{:S(2)}) %copy-start.3) | copy-done | bytes 1048
  21.0 0.0 copy-start.4
  21.0 0.7 %copy-done.4 = f32[256]{0:T(256)S(1)} copy-done((f32[256]{0:T(256)S(1)}, f32[256]{0:T(256)}, u32[]{:S(2)}) %copy-start.4) | copy-done | bytes 1048
  21.7 0.0 copy-start.5
  21.7 0.7 %copy-done.5 = f32[256]{0:T(256)S(1)} copy-done((f32[256]{0:T(256)S(1)}, f32[256]{0:T(256)}, u32[]{:S(2)}) %copy-start.5) | copy-done | bytes 1048
  22.4 0.0 copy-start.6
  22.4 0.7 %copy-done.6 = f32[256]{0:T(256)S(1)} copy-done((f32[256]{0:T(256)S(1)}, f32[256]{0:T(256)}, u32[]{:S(2)}) %copy-start.6) | copy-done | bytes 1048
  23.0 4.8 %shard_map.182 = (f32[8,1536]{1,0:T(8,128)S(1)}, bf16[256,1024]{1,0:T(8,128)(2,1)S(1)}, bf16[1024,256]{1,0:T(8,128)(2,1)S(1)}, bf16[256,512]{1,0:T(8,128)(2,1)S(...) custom-call(f32[12,8,4,512]{3,2,1,0:T(4,128)} %hidden_hbm.1, ...), custom_call_target="tpu_custom_call" | custom-call | flops 603979776 | bytes 8000000 | tf_op jit(solution)/shard_map/pallas_call | solution.py:523
  27.9 7.8 %all-to-all-done = bf16[128,32,128]{2,1,0:T(8,128)(2,1)S(1)} async-done(((bf16[128,32,128]{2,1,0:T(8,128)(2,1)}), bf16[128,32,128]{2,1,0:T(8,128)(2,1)S(1)}, u32[]{:S(2)}, u32[]{:S(2)}) %all-to-all-start) | async-done | bytes 1048608 | tf_op jit(solution)/shard_map/all_to_all | solution.py:600
  35.7 5.1 %shard_map.183 = f32[12,8,4,512]{3,2,1,0:T(4,128)} custom-call(bf16[4096,128]{1,0:T(8,128)(2,1)S(1)} %bitcast.11, f32[8,1536]{1,0:T(8,128)S(1)} %get-tuple-element.12.vector_ref, bf16[256,1024]{1,0:T(8,128)(2,1)S(1)} %get-tuple-element.13.expand_ref, bf16[1024,256]{1,0:T(8,128)(2,1)S(1)} %get-tuple-element.14.reduce_ref, ...), custom_call_target="tpu_custom_call" | custom-call | flops 1400000000 | bytes 8000000 | tf_op jit(solution)/shard_map/pallas_call | solution.py:553
Async XLA Ops:
  5.1 30.6 %all-to-all-start = ((bf16[128,32,128]{2,1,0:T(8,128)(2,1)}), bf16[128,32,128]{2,1,0:T(8,128)(2,1)S(1)}, u32[]{:S(2)}, u32[]{:S(2)}) async-start(bf16[128,32,128]{2,1,0:T(8,128)(2,1)} %bitcast.18), calls=%async_computation | async-start | bytes 2097152 | tf_op jit(solution)/shard_map/all_to_all | solution.py:600
  18.0 0.9 %copy-start = (bf16[256,512]{1,0:T(8,128)(2,1)S(1)}, bf16[256,512]{1,0:T(8,128)(2,1)}, u32[]{:S(2)}) copy-start(bf16[256,512]{1,0:T(8,128)(2,1)} %project_hbm.1) | copy-start | bytes 786436
  18.9 0.7 %copy-start.1 = (f32[1024]{0:T(1024)S(1)}, f32[1024]{0:T(1024)}, u32[]{:S(2)}) copy-start(f32[1024]{0:T(1024)} %param.27) | copy-start | bytes 12292
  19.6 0.7 %copy-start.2 = (f32[512]{0:T(512)S(1)}, f32[512]{0:T(512)}, u32[]{:S(2)}) copy-start(f32[512]{0:T(512)} %param.32) | copy-start | bytes 6148
  20.3 0.7 %copy-start.3 = (f32[256]{0:T(256)S(1)}, f32[256]{0:T(256)}, u32[]{:S(2)}) copy-start(f32[256]{0:T(256)} %param.24) | copy-start | bytes 3076
  21.0 0.7 %copy-start.4 = (f32[256]{0:T(256)S(1)}, f32[256]{0:T(256)}, u32[]{:S(2)}) copy-start(f32[256]{0:T(256)} %param.25) | copy-start | bytes 3076
  21.7 0.7 %copy-start.5 = (f32[256]{0:T(256)S(1)}, f32[256]{0:T(256)}, u32[]{:S(2)}) copy-start(f32[256]{0:T(256)} %param.29) | copy-start | bytes 3076
  22.4 0.7 %copy-start.6 = (f32[256]{0:T(256)S(1)}, f32[256]{0:T(256)}, u32[]{:S(2)}) copy-start(f32[256]{0:T(256)} %param.30) | copy-start | bytes 3076
